TPU v7x, 128 devices: a whole 4x4x4 slice. The times are simulated.
128 devices in a mesh: ccd: 16 (over y, x_hi, core), amp: 8 (over x_lo, z).
Axes of the slice: x: 4 (x_hi: 2, x_lo: 2; x = x_hi * 2 + x_lo), y: 4, z: 4, core: 2. Of those that a mesh axis runs over, the one named last changes fastest.
Arguments:
- science: float32 [16, 1024, 4096], P('ccd', 'amp'), may hold values from -6 to 6
- patches: float32 [16, 8, 4, 256, 256], P('ccd', 'amp'), may hold values from -6 to 6
- coeffs: float32 [16, 40, 6], P('ccd'), may hold values from -0.9 to 0.9
- tile_owner: int32 [16, 8, 32, 1], replicated, may hold values from 0 to 15; in each aligned block of 32 rows (0 to 31, 32 to 63, ..., all dimensions but the last counted through in order) at most 4 rows name the same one
- tile_patch: int32 [16, 8, 32], replicated, may hold values from 0 to 3
- tile_offset: int32 [16, 8, 32, 2], replicated, may hold values from 0 to 128
Outputs:
- difference: float32 [16, 1024, 4096], P('ccd', 'amp')
Inputs may be any that keep to these rules, and one draw needn't show every extreme that they name: `tile_owner`: among the 32 tiles of one strip, at most 4 name the same owner.
All inputs are finite; a program needn't handle non-finite values.
Results may differ from a plain program's by a relative error of at most 0.0031.
Values may be sent and summed in bfloat16 or wider, within the bound.
No kernel may reach another device: no remote copies, remote signals or barrier semaphores. Data moves between devices by JAX's collectives and lax.ppermute only.
A program may use at most 128 MiB of HBM per device.

v0:
```python
import numpy as np

import jax
import jax.numpy as jnp
import ml_dtypes
from jax import lax
from jax.experimental import pallas as pl
from jax.experimental.pallas import tpu as pltpu
from jax.sharding import PartitionSpec as P

TS = 128
HALF = 10
TAPS = 2 * HALF + 1
CAP = 4
WIDTHS = (1.0, 2.0, 4.0)
DEGREES = (4, 4, 3)
ROWS = 128
SIDE = 64
WIN = 80
EDGE = 16
K_MAIN = TAPS * WIN
K_PAD = 1792
K_EDGE = TAPS * EDGE
K_EDGE_PAD = 384
BLOCK = 512
TILES = BLOCK // TS
CUT = 16
MIB = 1 << 20


def factor_table():
    offsets = np.arange(-HALF, HALF + 1).astype(np.float64)
    shapes = []
    for width, degree in zip(WIDTHS, DEGREES):
        for power in range(degree + 1):
            profile = np.exp(-offsets * offsets / (2.0 * width * width)) * (offsets / HALF) ** power
            shapes.append(profile / np.sum(np.abs(profile)))
    return np.stack(shapes).astype(np.float32).astype(ml_dtypes.bfloat16).astype(np.float32)


def basis_table():
    factors = factor_table()
    rows = []
    first = 0
    for degree in DEGREES:
        for p in range(degree + 1):
            for q in range(degree + 1 - p):
                grid = np.zeros((TAPS, 128), np.float32)
                grid[:, :TAPS] = factors[first + p][:, None] * factors[first + q][None, :]
                rows.append(grid.reshape(-1))
        first += degree + 1
    return np.stack(rows)


def cut_kernel(table, patches, send, halves):
    step = pl.program_id(0)

    @pl.when(step == 0)
    def _():
        for patch in range(4):
            for side in range(2):
                at = (patch * 2 + side) * 256
                halves[at : at + 256, :] = patches[patch, :, side * TS : (side + 1) * TS]

    lane = lax.broadcasted_iota(jnp.int32, (TS, TS), 1)

    def tile(slot, carry):
        code = table[step * CUT + slot]
        at = ((code >> 4) & 3) * 512 + ((code >> 6) & 255)
        dx = (code >> 14) & 255
        turn = (TS - dx) & (TS - 1)
        low = pltpu.roll(halves[pl.ds(at, TS), :], turn, 1)
        high = pltpu.roll(halves[pl.ds(at + 256, TS), :], turn, 1)
        send[slot] = jnp.where(lane < TS - dx, low, high).astype(jnp.bfloat16)
        return carry

    lax.fori_loop(0, CUT, tile, 0, unroll=4)


def weights_kernel(amp, moments, main, edge):
    first_row = amp[0] * ROWS
    lane = lax.broadcasted_iota(jnp.int32, (SIDE, 128), 1)
    lane16 = lax.broadcasted_iota(jnp.int32, (EDGE, 128), 1)

    def across(rows, members, yh):
        total = jnp.broadcast_to(rows[members[0] : members[0] + 1], (yh.shape[0], 128))
        for power, member in enumerate(members[1:]):
            total = total + (yh if power == 0 else yh * yh) * rows[member : member + 1]
        return pltpu.roll(total, 0, 1, stride=1, stride_axis=0)

    for half in range(2):
        y = (first_row + half * SIDE + lax.broadcasted_iota(jnp.int32, (SIDE, 128), 0)).astype(jnp.float32)
        yh = (2.0 * y + 1.0) / 1024.0 - 1.0
        rim = slice(0, EDGE) if half == 0 else slice(SIDE - EDGE, SIDE)
        lead = 6 if half else -HALF
        rim_lead = EDGE - HALF if half == 0 else SIDE - EDGE + 6 - WIN
        for a, members in enumerate(((0, 2, 5), (1, 4), (3,))):
            held = jnp.zeros((SIDE, 128), jnp.float32)
            held_rim = jnp.zeros((EDGE, 128), jnp.float32)
            for u in range(TAPS):
                moment = moments[:, u * 128 : (u + 1) * 128]
                last = u == TAPS - 1
                group, low = u * WIN // 128, u * WIN % 128
                end = low + WIN
                turned = across(pltpu.roll(moment, (lead + low) % 128, 1), members, yh)
                held = jnp.where((lane >= low) & (lane < end), turned, held)
                at = slice(a * SIDE, (a + 1) * SIDE)
                if end >= 128 or last:
                    main[half, at, group * 128 : (group + 1) * 128] = held.astype(jnp.bfloat16)
                    held = jnp.where(lane < end - 128, turned, 0.0)
                    if last and end > 128:
                        main[half, at, (group + 1) * 128 : (group + 2) * 128] = held.astype(jnp.bfloat16)
                group, low = u * EDGE // 128, u * EDGE % 128
                turned = across(pltpu.roll(moment, (rim_lead + low) % 128, 1), members, yh[rim])
                held_rim = jnp.where((lane16 >= low) & (lane16 < low + EDGE), turned, held_rim)
                if low + EDGE == 128 or last:
                    at = slice(a * EDGE, (a + 1) * EDGE)
                    edge[half, at, group * 128 : (group + 1) * 128] = held_rim.astype(jnp.bfloat16)
                    held_rim = jnp.zeros((EDGE, 128), jnp.float32)


def edge_kernel(slots, tiles, top, bottom):
    for q in range(32):
        at = slice(q * TS, (q + 1) * TS)
        top[:, at] = tiles[slots[q], 0:EDGE, :]
        bottom[:, at] = tiles[slots[q], TS - EDGE : TS, :]


def x_of(first, shape):
    x = first + lax.broadcasted_iota(jnp.int32, shape, 1)
    return (2.0 * x.astype(jnp.float32) + 1.0) / 4096.0 - 1.0


def fold(parts, xh):
    rows = xh.shape[0]
    return parts[:rows] + xh * (parts[rows : 2 * rows] + xh * parts[2 * rows :])


def shifted_by(tiles, lag):
    if lag == 0:
        return tiles[1:-1]
    lane = lax.broadcasted_iota(jnp.int32, tiles[0].shape, 1)
    turned = [pltpu.roll(tile, (-lag) % TS, 1) for tile in tiles]
    if lag > 0:
        return [jnp.where(lane < TS - lag, turned[i], turned[i + 1]) for i in range(1, len(tiles) - 1)]
    return [jnp.where(lane < -lag, turned[i - 1], turned[i]) for i in range(1, len(tiles) - 1)]


def main_kernel(slots, tiles, weights, science, out, even, odd):
    step = pl.program_id(0)

    def shift(first, buffer):
        near = [tiles[slots[jnp.clip(first + i, 0, 31)]] for i in range(-1, TILES + 1)]
        near[0] = jnp.where(first > 0, near[0], jnp.zeros_like(near[0]))
        near[-1] = jnp.where(first + TILES < 32, near[-1], jnp.zeros_like(near[-1]))
        for u in range(TAPS):
            for i, tile in enumerate(shifted_by(near, u - HALF)):
                buffer[u, :, i * TS : (i + 1) * TS] = tile

    def multiply(first, buffer, columns):
        xh = x_of(first * TS, (SIDE, BLOCK))
        for half in range(2):
            source = buffer[:, half * 48 : half * 48 + WIN, :].reshape(K_MAIN, BLOCK)
            parts = jnp.dot(weights[half, :, :K_MAIN], source, preferred_element_type=jnp.float32)
            at = slice(half * SIDE, (half + 1) * SIDE)
            out[at, columns] = science[at, columns] - fold(parts, xh)

    @pl.when(step == 0)
    def _():
        shift(0, even)

    first = step * 2 * TILES
    shift(first + TILES, odd)
    multiply(first, even, slice(0, BLOCK))
    shift(first + 2 * TILES, even)
    multiply(first + TILES, odd, slice(BLOCK, 2 * BLOCK))


def rim_kernel(inner, above, below, weights, partial, out):
    step = pl.program_id(0)
    zero = jnp.zeros((EDGE, TS), jnp.bfloat16)

    def side(rows, number):
        keep = inner[number] > 0
        for first in range(0, 32, TILES):
            near = [
                rows[:, q * TS : (q + 1) * TS] if 0 <= q < 32 else zero for q in range(first - 1, first + TILES + 1)
            ]
            near = [jnp.where(keep, tile, zero) for tile in near]
            source = jnp.concatenate(
                [jnp.concatenate(shifted_by(near, u - HALF), axis=1) for u in range(TAPS)], axis=0
            )
            parts = jnp.dot(weights[number, :, :K_EDGE], source, preferred_element_type=jnp.float32)
            at = slice(first * TS, (first + TILES) * TS)
            out[:, at] = partial[:, at] - fold(parts, x_of(first * TS, (EDGE, BLOCK)))

    @pl.when(step == 0)
    def _():
        side(above, 0)

    @pl.when(step == 1)
    def _():
        side(below, 1)


def per_device(science, patches, coeffs, tile_owner, tile_patch, tile_offset):
    ccd_id = lax.axis_index("ccd")
    amp_id = lax.axis_index("amp")
    take = lambda array: lax.dynamic_index_in_dim(array, amp_id, 1, keepdims=False)
    shift = take(tile_offset)
    code = take(tile_owner)[..., 0] | (take(tile_patch) << 4) | (shift[..., 0] << 6) | (shift[..., 1] << 14)
    order = jnp.arange(32)
    named = code & 15
    chosen = named == ccd_id
    rank = jnp.sum((chosen[:, None, :] & (order[None, None, :] < order[None, :, None])).astype(jnp.int32), axis=2)
    place = chosen[:, None, :] & (rank[:, None, :] == jnp.arange(CAP)[None, :, None])
    table = jnp.sum(jnp.where(place, code[:, None, :], 0), axis=2).reshape(-1)

    whole = pl.BlockSpec(memory_space=pltpu.VMEM)
    scalars = pl.BlockSpec(memory_space=pltpu.SMEM)
    send = pl.pallas_call(
        cut_kernel,
        grid=(16 * CAP // CUT,),
        out_shape=jax.ShapeDtypeStruct((16 * CAP, TS, TS), jnp.bfloat16),
        in_specs=[scalars, whole],
        out_specs=pl.BlockSpec((CUT, TS, TS), lambda i: (i, 0, 0)),
        scratch_shapes=[pltpu.VMEM((4 * 2 * 256, TS), jnp.float32)],
        compiler_params=pltpu.CompilerParams(vmem_limit_bytes=24 * MIB),
        name="cut",
    )(table, patches.reshape(4, 256, 256))
    tiles = lax.all_to_all(send.reshape(16, CAP * TS, TS), "ccd", 0, 0, tiled=True).reshape(16 * CAP, TS, TS)

    mine = lax.dynamic_index_in_dim(named, ccd_id, 0, keepdims=False)
    earlier = (mine[:, None] == mine[None, :]) & (order[None, :] < order[:, None])
    slots = mine * CAP + jnp.minimum(jnp.sum(earlier.astype(jnp.int32), axis=1), CAP - 1)

    moments = jnp.einsum("km,kl->ml", coeffs[0], jnp.asarray(basis_table()), precision=lax.Precision.HIGHEST)
    main, edge = pl.pallas_call(
        weights_kernel,
        out_shape=(
            jax.ShapeDtypeStruct((2, 3 * SIDE, K_PAD), jnp.bfloat16),
            jax.ShapeDtypeStruct((2, 3 * EDGE, K_EDGE_PAD), jnp.bfloat16),
        ),
        in_specs=[scalars, whole],
        out_specs=(whole, whole),
        compiler_params=pltpu.CompilerParams(vmem_limit_bytes=24 * MIB),
        cost_estimate=pl.CostEstimate(flops=50_000_000, bytes_accessed=2_000_000, transcendentals=0),
        name="weights",
    )(amp_id.reshape(1), moments)

    top, bottom = pl.pallas_call(
        edge_kernel,
        out_shape=(jax.ShapeDtypeStruct((EDGE, 4096), jnp.bfloat16),) * 2,
        in_specs=[scalars, whole],
        out_specs=(whole, whole),
        compiler_params=pltpu.CompilerParams(vmem_limit_bytes=24 * MIB),
        name="edges",
    )(slots, tiles)
    down = [(i, i + 1) for i in range(7)]
    above = lax.ppermute(bottom, "amp", down)
    below = lax.ppermute(top, "amp", [(b, a) for a, b in down])

    columns = pl.BlockSpec((ROWS, 2 * BLOCK), lambda j, s: (0, j))
    partial = pl.pallas_call(
        main_kernel,
        grid_spec=pltpu.PrefetchScalarGridSpec(
            num_scalar_prefetch=1,
            grid=(4096 // (2 * BLOCK),),
            in_specs=[whole, whole, columns],
            out_specs=columns,
            scratch_shapes=[pltpu.VMEM((TAPS, ROWS, BLOCK), jnp.bfloat16)] * 2,
        ),
        out_shape=jax.ShapeDtypeStruct((ROWS, 4096), jnp.float32),
        compiler_params=pltpu.CompilerParams(vmem_limit_bytes=32 * MIB),
        cost_estimate=pl.CostEstimate(flops=11_000_000_000, bytes_accessed=8_000_000, transcendentals=0),
        name="main",
    )(slots, tiles, main, science[0])

    inner = jnp.stack([amp_id > 0, amp_id < 7]).astype(jnp.int32)
    strip_end = pl.BlockSpec((EDGE, 4096), lambda h, s: (7 * h, 0))
    result = pl.pallas_call(
        rim_kernel,
        grid_spec=pltpu.PrefetchScalarGridSpec(
            num_scalar_prefetch=1,
            grid=(2,),
            in_specs=[whole, whole, whole, strip_end],
            out_specs=strip_end,
        ),
        out_shape=jax.ShapeDtypeStruct((ROWS, 4096), jnp.float32),
        input_output_aliases={4: 0},
        compiler_params=pltpu.CompilerParams(vmem_limit_bytes=24 * MIB),
        name="rim",
    )(inner, above, below, edge, partial)
    return result[None]


def solution(mesh):
    placed = (
        P("ccd", "amp", None),
        P("ccd", "amp", None, None, None),
        P("ccd", None, None),
        P(),
        P(),
        P(),
    )
    return jax.shard_map(
        per_device, mesh=mesh, in_specs=placed, out_specs=P("ccd", "amp", None), check_vma=False
    )
```

profile of v0, /device:TPU:2, one launch (start us, length us, event | category | flops | bytes accessed | tf_op | source)
XLA Modules:
  0.0 69.9 jit_solution(6491490594323165743)
XLA Ops:
  0.0 0.9 %copy-done = s32[16,8,32,2]{2,3,1,0:T(2,128)S(1)} copy-done((s32[16,8,32,2]{2,3,1,0:T(2,128)S(1)}, s32[16,8,32,2]{2,3,1,0:T(2,128)}, u32[]{:S(2)}) %copy-start) | copy-done | bytes 32792
  0.9 0.9 %constant_dynamic-slice_fusion.5 = s32[16,1,32]{2,1,0:T(1,128)S(1)} fusion(s32[16,8,32]{2,1,0:T(8,128)} %param.11, s32[]{:T(128)S(6)} %select_n.16), kind=kLoop, calls=%fused_computation.24 | loop fusion | bytes 4100 | tf_op jit(solution)/shard_map/jit(dynamic_index_in_dim)/dynamic_slice | solution.py:209
  1.8 0.7 %constant_dynamic-slice_fusion.6 = s32[16,1,32,1]{2,3,1,0:T(1,128)S(1)} fusion(s32[16,8,32,1]{2,3,1,0:T(1,128)} %param.10, s32[]{:T(128)S(6)} %select_n.16), kind=kLoop, calls=%fused_computation.25 | loop fusion | bytes 4100 | tf_op jit(solution)/shard_map/jit(dynamic_index_in_dim)/dynamic_slice | solution.py:209
  2.5 0.4 convert_reduce_fusion
  2.8 0.1 select_reduce_fusion
  3.0 0.1 copy.14
  3.1 0.1 reshape.68.table
  3.2 0.0 copy-start.2
  3.2 1.2 %copy-done.2 = f32[1,1,4,256,256]{4,3,2,1,0:T(8,128)S(1)} copy-done((f32[1,1,4,256,256]{4,3,2,1,0:T(8,128)S(1)}, f32[1,1,4,256,256]{4,3,2,1,0:T(8,128)}, u32[]{:S(2)}) %copy-start.2) | copy-done | bytes 1048600
  4.4 2.9 %cut.1 = bf16[64,128,128]{2,1,0:T(8,128)(2,1)S(1)} custom-call(s32[64]{0:T(128)S(1)} %reshape.68.table, f32[4,256,256]{2,1,0:T(8,128)S(1)} %bitcast.42), custom_call_target="tpu_custom_call" | custom-call | tf_op jit(solution)/shard_map/cut/pallas_call | solution.py:221
  7.4 1.3 %copy-done.1 = bf16[64,128,128]{2,1,0:T(8,128)(2,1)} copy-done((bf16[64,128,128]{2,1,0:T(8,128)(2,1)}, bf16[64,128,128]{2,1,0:T(8,128)(2,1)S(1)}, u32[]{:S(2)}) %copy-start.1) | copy-done | bytes 2097176
  8.7 6.3 %all-to-all-start = ((bf16[16,512,128]{2,1,0:T(8,128)(2,1)}), bf16[16,512,128]{2,1,0:T(8,128)(2,1)S(1)}, u32[]{:S(2)}, u32[]{:S(2)}) async-start(bf16[16,512,128]{2,1,0:T(8,128)(2,1)} %bitcast.41), calls=%async_computation | async-start | bytes 4194304 | tf_op jit(solution)/shard_map/all_to_all | solution.py:231
  15.0 0.3 convolution_bitcast_fusion.moments
  15.3 17.6 %weights.1 = (bf16[2,192,1792]{2,1,0:T(8,128)(2,1)S(1)}, bf16[2,48,384]{2,1,0:T(8,128)(2,1)S(1)}) custom-call(s32[1]{0:T(128)} %bitcast.16.amp, f32[6,2688]{1,0:T(8,128)S(1)} %convolution_bitcast_fusion.moments), custom_call_target="tpu_custom_call" | custom-call | flops 50000000 | bytes 2000000 | tf_op jit(solution)/shard_map/weights/pallas_call | solution.py:238
  32.9 1.1 %copy-done.4 = bf16[2,192,1792]{2,1,0:T(8,128)(2,1)} copy-done((bf16[2,192,1792]{2,1,0:T(8,128)(2,1)}, bf16[2,192,1792]{2,1,0:T(8,128)(2,1)S(1)}, u32[]{:S(2)}) %copy-start.4) | copy-done | bytes 1376280
  34.0 0.1 add_convert_fusion.inner
  34.1 0.2 convert_reduce_fusion.1
  34.3 10.2 %all-to-all-done = bf16[16,512,128]{2,1,0:T(8,128)(2,1)S(1)} async-done(((bf16[16,512,128]{2,1,0:T(8,128)(2,1)}), bf16[16,512,128]{2,1,0:T(8,128)(2,1)S(1)}, u32[]{:S(2)}, u32[]{:S(2)}) %all-to-all-start) | async-done | bytes 2097184 | tf_op jit(solution)/shard_map/all_to_all | solution.py:231
  44.5 0.6 edges.1
  45.1 4.0 %collective-permute-start = (bf16[16,4096]{1,0:T(8,128)(2,1)S(1)}, bf16[16,4096]{1,0:T(8,128)(2,1)S(1)}, u32[]{:S(2)}, u32[]{:S(2)}) collective-permute-start(bf16[16,4096]{1,0:T(8,128)(2,1)S(1)} %get-tuple-element.9), channel_id=1, source_target_pairs={{0,1},{1,2},{2,3},{3,4},{4,5},{5,6},{6,7},{8,9},{9,10},{10,11},{11... | collective-permute-start | bytes 393224 | tf_op jit(solution)/shard_map/ppermute | solution.py:260
  49.1 4.6 %collective-permute-start.1 = (bf16[16,4096]{1,0:T(8,128)(2,1)S(1)}, bf16[16,4096]{1,0:T(8,128)(2,1)S(1)}, u32[]{:S(2)}, u32[]{:S(2)}) collective-permute-start(bf16[16,4096]{1,0:T(8,128)(2,1)S(1)} %get-tuple-element.10), channel_id=1, source_target_pairs={{1,0},{2,1},{3,2},{4,3},{5,4},{6,5},{7,6},{9,8},{10,9},{11,10},{12... | collective-permute-start | bytes 393224 | tf_op jit(solution)/shard_map/ppermute | solution.py:261
  53.8 1.3 %copy-done.5 = bf16[2,192,1792]{2,1,0:T(8,128)(2,1)S(1)} copy-done((bf16[2,192,1792]{2,1,0:T(8,128)(2,1)S(1)}, bf16[2,192,1792]{2,1,0:T(8,128)(2,1)}, u32[]{:S(2)}) %copy-start.5) | copy-done | bytes 1376280
  55.1 10.1 %main.1.partial = f32[128,4096]{1,0:T(8,128)} custom-call(s32[32]{0:T(128)S(1)} %minimum_add_fusion.slots, bf16[64,128,128]{2,1,0:T(8,128)(2,1)S(1)} %bitcast.40, bf16[2,192,1792]{2,1,0:T(8,128)(2,1)S(1)} %copy-done.5, f32[128,4096]{1,0:T(8,128)S(1)} %bitcast.43), custom_call_target="tpu_custom_call" | custom-call | flops 11000000512 | bytes 8000000 | tf_op jit(solution)/shard_map/main/pallas_call | solution.py:264
  65.2 4.7 %rim.1 = f32[128,4096]{1,0:T(8,128)} custom-call(s32[2]{0:T(128)S(1)} %add_convert_fusion.inner, bf16[16,4096]{1,0:T(8,128)(2,1)S(1)} %collective-permute-done.above, bf16[16,4096]{1,0:T(8,128)(2,1)S(1)} %collective-permute-done.1.below, bf16[2,48,384]{2,1,0:T(8,128)(2,1)S(1)} %get-tuple-element.11.weights, ...), custom_call_target="tpu_custom_call", output_to_operand_aliasing={{}: (4, {})} | custom-call | tf_op jit(solution)/shard_map/rim/pallas_call | solution.py:281
  (20 shorter events, 0.1 us)
Async XLA Ops:
  0.0 0.9 %copy-start = (s32[16,8,32,2]{2,3,1,0:T(2,128)S(1)}, s32[16,8,32,2]{2,3,1,0:T(2,128)}, u32[]{:S(2)}) copy-start(s32[16,8,32,2]{2,3,1,0:T(2,128)} %param.12) | copy-start | bytes 98308
  3.2 1.2 %copy-start.2 = (f32[1,1,4,256,256]{4,3,2,1,0:T(8,128)S(1)}, f32[1,1,4,256,256]{4,3,2,1,0:T(8,128)}, u32[]{:S(2)}) copy-start(f32[1,1,4,256,256]{4,3,2,1,0:T(8,128)} %param.8) | copy-start | bytes 3145732
  7.4 1.3 %copy-start.1 = (bf16[64,128,128]{2,1,0:T(8,128)(2,1)}, bf16[64,128,128]{2,1,0:T(8,128)(2,1)S(1)}, u32[]{:S(2)}) copy-start(bf16[64,128,128]{2,1,0:T(8,128)(2,1)S(1)} %cut.1) | copy-start | bytes 6291460
  8.7 6.3 %copy-start.6 = (f32[40,2688]{1,0:T(8,128)S(1)}, f32[40,2688]{1,0:T(8,128)}, u32[]{:S(2)}) copy-start(f32[40,2688]{1,0:T(8,128)} %constant.44.clone) | copy-start | bytes 1290244
  8.7 6.3 %copy-start.7 = (f32[1,40,6]{1,0,2:T(1,128)S(1)}, f32[1,40,6]{1,0,2:T(1,128)}, u32[]{:S(2)}) copy-start(f32[1,40,6]{1,0,2:T(1,128)} %param.9) | copy-start | bytes 2884
  8.7 35.9 %all-to-all-start = ((bf16[16,512,128]{2,1,0:T(8,128)(2,1)}), bf16[16,512,128]{2,1,0:T(8,128)(2,1)S(1)}, u32[]{:S(2)}, u32[]{:S(2)}) async-start(bf16[16,512,128]{2,1,0:T(8,128)(2,1)} %bitcast.41), calls=%async_computation | async-start | bytes 4194304 | tf_op jit(solution)/shard_map/all_to_all | solution.py:231
  32.9 1.1 %copy-start.4 = (bf16[2,192,1792]{2,1,0:T(8,128)(2,1)}, bf16[2,192,1792]{2,1,0:T(8,128)(2,1)S(1)}, u32[]{:S(2)}) copy-start(bf16[2,192,1792]{2,1,0:T(8,128)(2,1)S(1)} %get-tuple-element.12.weights) | copy-start | bytes 4128772
  44.5 9.2 %copy-start.3 = (f32[1,128,4096]{2,1,0:T(8,128)S(1)}, f32[1,128,4096]{2,1,0:T(8,128)}, u32[]{:S(2)}) copy-start(f32[1,128,4096]{2,1,0:T(8,128)} %param.7) | copy-start | bytes 6291460
  45.1 20.1 %collective-permute-start = (bf16[16,4096]{1,0:T(8,128)(2,1)S(1)}, bf16[16,4096]{1,0:T(8,128)(2,1)S(1)}, u32[]{:S(2)}, u32[]{:S(2)}) collective-permute-start(bf16[16,4096]{1,0:T(8,128)(2,1)S(1)} %get-tuple-element.9), channel_id=1, source_target_pairs={{0,1},{1,2},{2,3},{3,4},{4,5},{5,6},{6,7},{8,9},{9,10},{10,11},{11... | collective-permute-start | bytes 393224 | tf_op jit(solution)/shard_map/ppermute | solution.py:260
  49.1 16.1 %collective-permute-start.1 = (bf16[16,4096]{1,0:T(8,128)(2,1)S(1)}, bf16[16,4096]{1,0:T(8,128)(2,1)S(1)}, u32[]{:S(2)}, u32[]{:S(2)}) collective-permute-start(bf16[16,4096]{1,0:T(8,128)(2,1)S(1)} %get-tuple-element.10), channel_id=1, source_target_pairs={{1,0},{2,1},{3,2},{4,3},{5,4},{6,5},{7,6},{9,8},{10,9},{11,10},{12... | collective-permute-start | bytes 393224 | tf_op jit(solution)/shard_map/ppermute | solution.py:261
  53.8 1.3 %copy-start.5 = (bf16[2,192,1792]{2,1,0:T(8,128)(2,1)S(1)}, bf16[2,192,1792]{2,1,0:T(8,128)(2,1)}, u32[]{:S(2)}) copy-start(bf16[2,192,1792]{2,1,0:T(8,128)(2,1)} %copy-done.4) | copy-start | bytes 4128772
where the time goes:
time: 70.3 us; the launch traced here: 69.9 us
  Pallas kernels  35.9 us (51%)
  starting transfers between devices  14.9 us (21%)
  waiting for transfers between devices  10.2 us (15%)
  local copies, waits for them, and re-layouts  7.62 us (11%)
  other arithmetic  0.8 us (1%)
    pallas_call x1, Pallas kernels, per_device(): pl.pallas_call(weights_kernel, out_shape=(jax.ShapeDtypeStruct((2, 3 * SI...  17.6 us
    all_to_all x1, waiting for transfers between devices, per_device(): lax.all_to_all(send.reshape(16, CAP * TS, TS), 'ccd', 0, 0, tiled=True)  10.2 us
    pallas_call x1, Pallas kernels, per_device(): pl.pallas_call(main_kernel, grid_spec=pltpu.PrefetchScalarGridSpec(num_sc...  10.1 us
    all_to_all x1, starting transfers between devices, per_device(): lax.all_to_all(send.reshape(16, CAP * TS, TS), 'ccd', 0, 0, tiled=True)  6.27 us
    unnamed x17, local copies, waits for them, and re-layouts  5.88 us
    pallas_call x1, Pallas kernels, per_device(): pl.pallas_call(rim_kernel, grid_spec=pltpu.PrefetchScalarGridSpec(num_sca...  4.68 us
    ppermute x1, starting transfers between devices, per_device(): below = lax.ppermute(top, 'amp', [(b, a) for a, b in down])  4.63 us
    ppermute x1, starting transfers between devices, per_device(): above = lax.ppermute(bottom, 'amp', down)  3.96 us
  transfers between devices with their start and end apart: 3, of which 1 were waited for; matrix products, arithmetic and copies ran while one was open for 1% of the time, Pallas kernels for 40%

commit v1 on v0

v1 whole, which is shorter than its diff:
```python
import numpy as np

import jax
import jax.numpy as jnp
import ml_dtypes
from jax import lax
from jax.experimental import pallas as pl
from jax.experimental.pallas import tpu as pltpu
from jax.sharding import PartitionSpec as P

TS = 128
HALF = 10
TAPS = 2 * HALF + 1
CAP = 4
WIDTHS = (1.0, 2.0, 4.0)
DEGREES = (4, 4, 3)
ROWS = 128
SIDE = 64
WIN = 80
EDGE = 16
K_MAIN = (TAPS + 1) * WIN
K_PAD = 1792
K_EDGE = (TAPS + 1) * EDGE
K_EDGE_PAD = 384
BLOCK = 512
WIDE = BLOCK // 2
TILES = WIDE // TS
LAGS = TAPS + 1
CUT = 16
MIB = 1 << 20


def factor_table():
    offsets = np.arange(-HALF, HALF + 1).astype(np.float64)
    shapes = []
    for width, degree in zip(WIDTHS, DEGREES):
        for power in range(degree + 1):
            profile = np.exp(-offsets * offsets / (2.0 * width * width)) * (offsets / HALF) ** power
            shapes.append(profile / np.sum(np.abs(profile)))
    return np.stack(shapes).astype(np.float32).astype(ml_dtypes.bfloat16).astype(np.float32)


def basis_table():
    factors = factor_table()
    rows = []
    first = 0
    for degree in DEGREES:
        for p in range(degree + 1):
            for q in range(degree + 1 - p):
                grid = np.zeros((TAPS, 128), np.float32)
                grid[:, :TAPS] = factors[first + p][:, None] * factors[first + q][None, :]
                rows.append(grid.reshape(-1))
        first += degree + 1
    return np.stack(rows)


def cut_kernel(here, codes, patches, send, halves, listed, table, sems, table_sem):
    step = pl.program_id(0)

    @pl.when(step == 0)
    def _():
        copies = [
            pltpu.make_async_copy(
                patches.at[patch, :, pl.ds(side * TS, TS)],
                halves.at[pl.ds((patch * 2 + side) * 256, 256), :],
                sems.at[patch, side],
            )
            for patch in range(4)
            for side in range(2)
        ]
        for copy in copies:
            copy.start()
        code = codes[here[0]]
        mine = (code & 15) == here[1]
        earlier = lax.broadcasted_iota(jnp.int32, (32, 32), 0) < lax.broadcasted_iota(jnp.int32, (32, 32), 1)
        as_bf16 = lambda mask: mask.astype(jnp.float32).astype(jnp.bfloat16)
        rank = jnp.dot(as_bf16(mine), as_bf16(earlier), preferred_element_type=jnp.float32)
        code = code.astype(jnp.float32)
        lane = lax.broadcasted_iota(jnp.int32, (16, 128), 1)
        total = jnp.zeros((16, 128), jnp.float32)
        for k in range(CAP):
            found = jnp.sum(jnp.where(mine & (rank == k), code, 0.0), axis=1, keepdims=True)
            total = jnp.where(lane == k, found, total)
        listed[...] = total.astype(jnp.int32)
        copy = pltpu.make_async_copy(listed, table, table_sem)
        copy.start()
        copy.wait()
        for copy in copies:
            copy.wait()

    lane = lax.broadcasted_iota(jnp.int32, (TS, TS), 1)

    def tile(slot, carry):
        code = table[step * (CUT // CAP) + slot // CAP, slot % CAP]
        at = ((code >> 4) & 3) * 512 + ((code >> 6) & 255)
        dx = (code >> 14) & 255
        turn = (TS - dx) & (TS - 1)
        low = pltpu.roll(halves[pl.ds(at, TS), :], turn, 1)
        high = pltpu.roll(halves[pl.ds(at + 256, TS), :], turn, 1)
        send[slot] = jnp.where(lane < TS - dx, low, high).astype(jnp.bfloat16)
        return carry

    lax.fori_loop(0, CUT, tile, 0, unroll=4)


def weights_kernel(amp, moments, main, edge):
    first_row = amp[0] * ROWS
    lane = lax.broadcasted_iota(jnp.int32, (SIDE, 128), 1)
    lane16 = lax.broadcasted_iota(jnp.int32, (EDGE, 128), 1)

    def across(rows, members, yh):
        total = jnp.broadcast_to(rows[members[0] : members[0] + 1], (yh.shape[0], 128))
        for power, member in enumerate(members[1:]):
            total = total + (yh if power == 0 else yh * yh) * rows[member : member + 1]
        return pltpu.roll(total, 0, 1, stride=1, stride_axis=0)

    for half in range(2):
        y = (first_row + half * SIDE + lax.broadcasted_iota(jnp.int32, (SIDE, 128), 0)).astype(jnp.float32)
        yh = (2.0 * y + 1.0) / 1024.0 - 1.0
        rim = slice(0, EDGE) if half == 0 else slice(SIDE - EDGE, SIDE)
        lead = 6 if half else -HALF
        rim_lead = EDGE - HALF if half == 0 else SIDE - EDGE + 6 - WIN
        for a, members in enumerate(((0, 2, 5), (1, 4), (3,))):
            held = jnp.zeros((SIDE, 128), jnp.float32)
            held_rim = jnp.zeros((EDGE, 128), jnp.float32)
            for u in range(TAPS):
                moment = moments[:, u * 128 : (u + 1) * 128]
                last = u == TAPS - 1
                group, low = u * WIN // 128, u * WIN % 128
                end = low + WIN
                turned = across(pltpu.roll(moment, (lead + low) % 128, 1), members, yh)
                held = jnp.where((lane >= low) & (lane < end), turned, held)
                at = slice(a * SIDE, (a + 1) * SIDE)
                if end >= 128 or last:
                    main[half, at, group * 128 : (group + 1) * 128] = held.astype(jnp.bfloat16)
                    held = jnp.where(lane < end - 128, turned, 0.0)
                    if last and end > 128:
                        main[half, at, (group + 1) * 128 : (group + 2) * 128] = held.astype(jnp.bfloat16)
                group, low = u * EDGE // 128, u * EDGE % 128
                turned = across(pltpu.roll(moment, (rim_lead + low) % 128, 1), members, yh[rim])
                held_rim = jnp.where((lane16 >= low) & (lane16 < low + EDGE), turned, held_rim)
                if low + EDGE == 128 or last:
                    at = slice(a * EDGE, (a + 1) * EDGE)
                    edge[half, at, group * 128 : (group + 1) * 128] = held_rim.astype(jnp.bfloat16)
                    held_rim = jnp.zeros((EDGE, 128), jnp.float32)
        main[half, 3 * SIDE :, :] = pltpu.roll(main[half, : 3 * SIDE, :], WIN, 1)
        edge[half, 3 * EDGE :, :] = pltpu.roll(edge[half, : 3 * EDGE, :], EDGE, 1)


def apart(transposed):
    wide, narrow = (1, 0) if transposed else (0, 1)
    column = lax.broadcasted_iota(jnp.int32, (256, 256), wide)
    place = lax.broadcasted_iota(jnp.int32, (256, 256), narrow)
    home = jnp.where(place < TS, 2 * place, 2 * place - 255)
    return (column == home).astype(jnp.float32).astype(jnp.bfloat16)


def phase_kernel(slots, tiles, planes, top, bottom):
    split = apart(False)
    for pair in range(16):
        both = jnp.concatenate([tiles[slots[2 * pair]], tiles[slots[2 * pair + 1]]], axis=1)
        moved = jnp.dot(both, split, preferred_element_type=jnp.float32).astype(jnp.bfloat16)
        for phase in range(2):
            piece = moved[:, phase * TS : (phase + 1) * TS]
            planes[phase, :, pair * TS : (pair + 1) * TS] = piece
            at = slice(phase * 2048 + pair * TS, phase * 2048 + (pair + 1) * TS)
            top[:, at] = piece[:EDGE]
            bottom[:, at] = piece[TS - EDGE :]


def fold(parts, first, rows):
    folded = []
    for phase in range(2):
        x = 2 * (first + lax.broadcasted_iota(jnp.int32, (rows, parts.shape[1]), 1)) + phase
        xh = (2.0 * x.astype(jnp.float32) + 1.0) / 4096.0 - 1.0
        terms = [parts[(phase * 3 + a) * rows : (phase * 3 + a + 1) * rows] for a in range(3)]
        folded.append(terms[0] + xh * (terms[1] + xh * terms[2]))
    return folded


def together(pieces, join):
    rows = pieces[0].shape[0]
    both = jnp.concatenate(pieces, axis=0)
    high = both.astype(jnp.bfloat16)
    low = (both - high.astype(jnp.float32)).astype(jnp.bfloat16)
    moved = jnp.dot(jnp.concatenate([high, low], axis=0), join, preferred_element_type=jnp.float32)
    moved = moved[: both.shape[0]] + moved[both.shape[0] :]
    return [moved[i * rows : (i + 1) * rows] for i in range(len(pieces))]


def paired(folded, i):
    return jnp.concatenate([phase[:, i * TS : (i + 1) * TS] for phase in folded], axis=1)


def shifted_by(tiles, lag):
    if lag == 0:
        return tiles[1:-1]
    lane = lax.broadcasted_iota(jnp.int32, tiles[0].shape, 1)
    turned = [pltpu.roll(tile, (-lag) % TS, 1) for tile in tiles]
    if lag > 0:
        return [jnp.where(lane < TS - lag, turned[i], turned[i + 1]) for i in range(1, len(tiles) - 1)]
    return [jnp.where(lane < -lag, turned[i - 1], turned[i]) for i in range(1, len(tiles) - 1)]


def main_kernel(planes, weights, science, out, even, odd, held, sems):
    step = pl.program_id(0)
    copies = [
        pltpu.make_async_copy(weights.at[half, pl.ds(part * 96, 96)], held.at[half, pl.ds(part * 96, 96)], sems.at[half, part])
        for half in range(2)
        for part in range(4)
    ]

    def shift(first, buffer):
        near = []
        for phase in range(2):
            tiles = [
                planes[phase, :, pl.ds(pl.multiple_of(jnp.clip(first + i, 0, 15) * TS, TS), TS)] for i in range(-1, TILES + 1)
            ]
            tiles[0] = jnp.where(first > 0, tiles[0], jnp.zeros_like(tiles[0]))
            tiles[-1] = jnp.where(first + TILES < 16, tiles[-1], jnp.zeros_like(tiles[-1]))
            near.append(tiles)
        for index in range(LAGS):
            lag = index - HALF
            for i, tile in enumerate(shifted_by(near[lag % 2], lag // 2)):
                buffer[index, :, i * TS : (i + 1) * TS] = tile

    def multiply(first, buffer):
        pieces = []
        for half in range(2):
            source = buffer[:, half * 48 : half * 48 + WIN, :].reshape(K_MAIN, WIDE)
            parts = jnp.dot(held[half, :, :K_MAIN], source, preferred_element_type=jnp.float32)
            folded = fold(parts, first * TS, SIDE)
            pieces += [paired(folded, i) for i in range(TILES)]
        return pieces

    @pl.when(step == 0)
    def _():
        for copy in copies:
            copy.start()
        shift(0, even)
        for copy in copies:
            copy.wait()

    first = step * 2 * TILES
    shift(first + TILES, odd)
    pieces = multiply(first, even)
    shift(first + 2 * TILES, even)
    pieces += multiply(first + TILES, odd)
    for n, model in enumerate(together(pieces, apart(True))):
        block, half, i = n // (2 * TILES), n // TILES % 2, n % TILES
        at = slice(half * SIDE, (half + 1) * SIDE)
        columns = slice(block * BLOCK + i * 256, block * BLOCK + (i + 1) * 256)
        out[at, columns] = science[at, columns] - model


def rim_kernel(inner, above, below, weights, partial, out, shifted, ends, sems):
    zero = jnp.zeros((EDGE, TS), jnp.bfloat16)
    rows = [pl.ds(0, EDGE), pl.ds(ROWS - EDGE, EDGE)]
    for number in range(2):
        pltpu.make_async_copy(partial.at[rows[number]], ends.at[number], sems.at[0, number]).start()
    pieces = []
    for number, source in enumerate((above, below)):
        keep = inner[number] > 0
        near = []
        for phase in range(2):
            tiles = [source[:, phase * 2048 + i * TS : phase * 2048 + (i + 1) * TS] for i in range(16)]
            near.append([zero] + [jnp.where(keep, tile, zero) for tile in tiles] + [zero])
        for index in range(LAGS):
            lag = index - HALF
            for i, tile in enumerate(shifted_by(near[lag % 2], lag // 2)):
                shifted[number, index, :, i * TS : (i + 1) * TS] = tile
        for first in range(0, 16, 4):
            lags = shifted[number, :, :, first * TS : (first + 4) * TS].reshape(K_EDGE, 4 * TS)
            parts = jnp.dot(weights[number, :, :K_EDGE], lags, preferred_element_type=jnp.float32)
            folded = fold(parts, first * TS, EDGE)
            pieces += [paired(folded, i) for i in range(4)]
    models = together(pieces, apart(True))
    for number in range(2):
        pltpu.make_async_copy(partial.at[rows[number]], ends.at[number], sems.at[0, number]).wait()
        for i in range(16):
            at = slice(i * 256, (i + 1) * 256)
            ends[number, :, at] = ends[number, :, at] - models[number * 16 + i]
        pltpu.make_async_copy(ends.at[number], out.at[rows[number]], sems.at[1, number]).start()
    for number in range(2):
        pltpu.make_async_copy(ends.at[number], out.at[rows[number]], sems.at[1, number]).wait()


def per_device(science, patches, coeffs, tile_owner, tile_patch, tile_offset):
    ccd_id = lax.axis_index("ccd")
    amp_id = lax.axis_index("amp")
    codes = tile_owner[..., 0] | (tile_patch << 4) | (tile_offset[..., 0] << 6) | (tile_offset[..., 1] << 14)
    codes = codes.transpose(1, 0, 2)
    here = jnp.stack([amp_id, ccd_id])

    whole = pl.BlockSpec(memory_space=pltpu.VMEM)
    scalars = pl.BlockSpec(memory_space=pltpu.SMEM)
    send = pl.pallas_call(
        cut_kernel,
        grid=(16 * CAP // CUT,),
        out_shape=pltpu.HBM((16 * CAP, TS, TS), jnp.bfloat16),
        in_specs=[scalars, whole, pl.BlockSpec(memory_space=pl.ANY)],
        out_specs=pl.BlockSpec((CUT, TS, TS), lambda i: (i, 0, 0)),
        scratch_shapes=[
            pltpu.VMEM((4 * 2 * 256, TS), jnp.float32),
            pltpu.VMEM((16, 128), jnp.int32),
            pltpu.SMEM((16, 128), jnp.int32),
            pltpu.SemaphoreType.DMA((4, 2)),
            pltpu.SemaphoreType.DMA,
        ],
        compiler_params=pltpu.CompilerParams(vmem_limit_bytes=10 * MIB),
        name="cut",
    )(here, codes, pltpu.with_memory_space_constraint(patches.reshape(4, 256, 256), pltpu.HBM))
    tiles = lax.all_to_all(send.reshape(16, CAP * TS, TS), "ccd", 0, 0, tiled=True).reshape(16 * CAP, TS, TS)

    order = jnp.arange(32)
    mine = tile_owner[ccd_id, amp_id, :, 0]
    earlier = (mine[:, None] == mine[None, :]) & (order[None, :] < order[:, None])
    slots = mine * CAP + jnp.minimum(jnp.sum(earlier.astype(jnp.int32), axis=1), CAP - 1)

    moments = jnp.einsum("km,kl->ml", coeffs[0], jnp.asarray(basis_table()), precision=lax.Precision.HIGHEST)
    main, edge = pl.pallas_call(
        weights_kernel,
        out_shape=(
            pltpu.HBM((2, 6 * SIDE, K_PAD), jnp.bfloat16),
            jax.ShapeDtypeStruct((2, 6 * EDGE, K_EDGE_PAD), jnp.bfloat16),
        ),
        in_specs=[scalars, whole],
        out_specs=(whole, whole),
        compiler_params=pltpu.CompilerParams(vmem_limit_bytes=10 * MIB),
        cost_estimate=pl.CostEstimate(flops=50_000_000, bytes_accessed=2_000_000, transcendentals=0),
        name="weights",
    )(amp_id.reshape(1), moments)

    planes, top, bottom = pl.pallas_call(
        phase_kernel,
        out_shape=(jax.ShapeDtypeStruct((2, ROWS, 2048), jnp.bfloat16),)
        + (jax.ShapeDtypeStruct((EDGE, 4096), jnp.bfloat16),) * 2,
        in_specs=[scalars, whole],
        out_specs=(whole, whole, whole),
        compiler_params=pltpu.CompilerParams(vmem_limit_bytes=8 * MIB),
        name="phases",
    )(slots, tiles)
    down = [(i, i + 1) for i in range(7)]
    above = lax.ppermute(bottom, "amp", down)
    below = lax.ppermute(top, "amp", [(b, a) for a, b in down])

    columns = pl.BlockSpec((ROWS, 2 * BLOCK), lambda j: (0, j))
    partial = pl.pallas_call(
        main_kernel,
        grid=(4096 // (2 * BLOCK),),
        in_specs=[whole, pl.BlockSpec(memory_space=pl.ANY), columns],
        out_specs=columns,
        scratch_shapes=[pltpu.VMEM((LAGS, ROWS, WIDE), jnp.bfloat16)] * 2
        + [pltpu.VMEM((2, 6 * SIDE, K_PAD), jnp.bfloat16), pltpu.SemaphoreType.DMA((2, 4))],
        out_shape=jax.ShapeDtypeStruct((ROWS, 4096), jnp.float32),
        compiler_params=pltpu.CompilerParams(vmem_limit_bytes=24 * MIB),
        cost_estimate=pl.CostEstimate(flops=11_000_000_000, bytes_accessed=8_000_000, transcendentals=0),
        name="main",
    )(planes, pltpu.with_memory_space_constraint(main, pltpu.HBM), science[0])

    inner = jnp.stack([amp_id > 0, amp_id < 7]).astype(jnp.int32)
    result = pl.pallas_call(
        rim_kernel,
        in_specs=[scalars, whole, whole, whole, pl.BlockSpec(memory_space=pl.ANY)],
        out_specs=pl.BlockSpec(memory_space=pl.ANY),
        scratch_shapes=[
            pltpu.VMEM((2, LAGS, EDGE, 2048), jnp.bfloat16),
            pltpu.VMEM((2, EDGE, 4096), jnp.float32),
            pltpu.SemaphoreType.DMA((2, 2)),
        ],
        out_shape=jax.ShapeDtypeStruct((ROWS, 4096), jnp.float32),
        input_output_aliases={4: 0},
        compiler_params=pltpu.CompilerParams(vmem_limit_bytes=16 * MIB),
        name="rim",
    )(inner, above, below, edge, partial)
    return result[None]


def solution(mesh):
    placed = (
        P("ccd", "amp", None),
        P("ccd", "amp", None, None, None),
        P("ccd", None, None),
        P(),
        P(),
        P(),
    )
    return jax.shard_map(
        per_device, mesh=mesh, in_specs=placed, out_specs=P("ccd", "amp", None), check_vma=False
    )
```

time: 70.3 us -> 66.4 us (0.945)
  local copies, waits for them, and re-layouts: 7.62 us -> 1.77 us
  Pallas kernels: 35.9 us -> 39.7 us
  waiting for transfers between devices: 10.2 us -> 7.42 us
  other arithmetic: 0.8 us -> 1.92 us
    unnamed x17 -> x6, local copies, waits for them, and re-layouts: 5.88 us -> 0.02 us
    pallas_call x5, Pallas kernels: 35.9 us -> 39.7 us  [the longest x1 20.2 us: per_device(): pl.pallas_call(weights_kernel, out_shape=(pltpu.HBM((2, 6 * SIDE, K_PAD),...]
    all_to_all x1, waiting for transfers between devices: 10.2 us -> 7.42 us  [per_device(): lax.all_to_all(send.reshape(16, CAP * TS, TS), 'ccd', 0, 0, tiled=True)]
    dynamic_slice x3 -> x0, local copies, waits for them, and re-layouts: 1.56 us -> none  [per_device(): lax.dynamic_index_in_dim(array, amp_id, 1, keepdims=False)]
    slice x0 -> x1, local copies, waits for them, and re-layouts: none -> 1.09 us  [per_device(): tile_offset[..., 0] << 6]
    transpose x0 -> x1, other arithmetic: none -> 0.92 us  [per_device(): codes = codes.transpose(1, 0, 2)]
  transfers between devices with their start and end apart: 3 -> 3, of which waited for: 1 -> 1; matrix products, arithmetic and copies ran while one was open for 1% -> 3% of each run, Pallas kernels for 40% -> 46%
where the time goes in v1:
time: 66.4 us; the launch traced here: 66 us
  Pallas kernels  39.7 us (60%)
  starting transfers between devices  14.7 us (22%)
  waiting for transfers between devices  7.42 us (11%)
  other arithmetic  1.92 us (3%)
  local copies, waits for them, and re-layouts  1.77 us (3%)
    pallas_call x1, Pallas kernels, per_device(): pl.pallas_call(weights_kernel, out_shape=(pltpu.HBM((2, 6 * SIDE, K_PAD),...  20.2 us
    pallas_call x1, Pallas kernels, per_device(): pl.pallas_call(main_kernel, grid=(4096 // (2 * BLOCK),), in_specs=[whole,...  10.3 us
    all_to_all x1, waiting for transfers between devices, per_device(): lax.all_to_all(send.reshape(16, CAP * TS, TS), 'ccd', 0, 0, tiled=True)  7.42 us
    all_to_all x1, starting transfers between devices, per_device(): lax.all_to_all(send.reshape(16, CAP * TS, TS), 'ccd', 0, 0, tiled=True)  6.28 us
    pallas_call x1, Pallas kernels, per_device(): pl.pallas_call(cut_kernel, grid=(16 * CAP // CUT,), out_shape=pltpu.HBM((...  5.33 us
    ppermute x1, starting transfers between devices, per_device(): below = lax.ppermute(top, 'amp', [(b, a) for a, b in down])  4.64 us
    ppermute x1, starting transfers between devices, per_device(): above = lax.ppermute(bottom, 'amp', down)  3.83 us
    pallas_call x1, Pallas kernels, per_device(): pl.pallas_call(rim_kernel, in_specs=[scalars, whole, whole, whole, pl.Blo...  2.86 us
  transfers between devices with their start and end apart: 3, of which 1 were waited for; matrix products, arithmetic and copies ran while one was open for 3% of the time, Pallas kernels for 46%

profile of v1, /device:TPU:2, one launch (start us, length us, event | category | flops | bytes accessed | tf_op | source)
XLA Modules:
  0.0 66.0 jit_solution(3596809552891640474)
XLA Ops:
  0.0 1.1 %fusion.6 = (s32[16,8,32,1]{2,3,1,0:T(1,128)S(1)}, s32[16,8,32,1]{2,3,1,0:T(1,128)S(1)}) fusion(s32[16,8,32,2]{2,3,1,0:T(2,128)} %param.12), kind=kLoop, calls=%fused_computation.18 | loop fusion | bytes 65536 | tf_op jit(solution)/shard_map/slice | solution.py:291
  1.1 0.1 pad_add_fusion.here
  1.2 0.9 %fusion.2.codes = s32[8,16,32]{2,1,0:T(8,128)S(1)} fusion(s32[16,8,32,1]{2,3,1,0:T(1,128)S(1)} %get-tuple-element.16, s32[16,8,32,1]{2,3,1,0:T(1,128)S(1)} %get-tuple-element.15, s32[16,8,32]{2,1,0:T(8,128)} %param.11, s32[16,8,32,1]{2,3,1,0:T(1,128)} %param.10), kind=kLoop, calls=%fused_computation.4 | loop fusion | flops 24576 | bytes 81920 | tf_op jit(solution)/shard_map/transpose | solution.py:292
  2.1 5.3 %cut.1 = bf16[64,128,128]{2,1,0:T(8,128)(2,1)} custom-call(s32[2]{0:T(128)S(1)} %pad_add_fusion.here, s32[8,16,32]{2,1,0:T(8,128)S(1)} %fusion.2.codes, f32[4,256,256]{2,1,0:T(8,128)} %bitcast.40), custom_call_target="tpu_custom_call" | custom-call | tf_op jit(solution)/shard_map/cut/pallas_call | solution.py:297
  7.4 0.0 copy-start.1
  7.4 0.0 copy-start.2
  7.5 6.3 %all-to-all-start = ((bf16[16,512,128]{2,1,0:T(8,128)(2,1)}), bf16[16,512,128]{2,1,0:T(8,128)(2,1)S(1)}, u32[]{:S(2)}, u32[]{:S(2)}) async-start(bf16[16,512,128]{2,1,0:T(8,128)(2,1)} %bitcast.39), calls=%async_computation | async-start | bytes 4194304 | tf_op jit(solution)/shard_map/all_to_all | solution.py:313
  13.8 0.0 copy-done.1
  13.8 0.0 copy-done.2
  13.8 0.3 convolution_bitcast_fusion.moments
  14.1 20.2 %weights.1 = (bf16[2,384,1792]{2,1,0:T(8,128)(2,1)}, bf16[2,96,384]{2,1,0:T(8,128)(2,1)S(1)}) custom-call(s32[1]{0:T(128)} %bitcast.3.amp, f32[6,2688]{1,0:T(8,128)S(1)} %convolution_bitcast_fusion.moments), custom_call_target="tpu_custom_call" | custom-call | flops 50000000 | bytes 2000000 | tf_op jit(solution)/shard_map/weights/pallas_call | solution.py:321
  34.3 0.1 add_convert_fusion.inner
  34.4 0.7 dynamic-slice_bitcast_fusion
  35.1 0.2 convert_reduce_fusion
  35.2 0.7 %minimum_add_fusion.slots = s32[32]{0:T(128)S(1)} fusion(s32[32]{0:T(128)S(1)} %convert_reduce_fusion, s32[16,8,32,1]{2,3,1,0:T(1,128)} %param.10, s32[]{:T(128)S(6)} %select_n.6, s32[]{:T(128)S(6)} %select_n.7), kind=kLoop, calls=%fused_computation.16 | loop fusion | flops 96 | bytes 392 | tf_op jit(solution)/shard_map/add | solution.py:318
  35.9 7.4 %all-to-all-done = bf16[16,512,128]{2,1,0:T(8,128)(2,1)S(1)} async-done(((bf16[16,512,128]{2,1,0:T(8,128)(2,1)}), bf16[16,512,128]{2,1,0:T(8,128)(2,1)S(1)}, u32[]{:S(2)}, u32[]{:S(2)}) %all-to-all-start) | async-done | bytes 2097184 | tf_op jit(solution)/shard_map/all_to_all | solution.py:313
  43.3 1.0 %phases.1 = (bf16[2,128,2048]{2,1,0:T(8,128)(2,1)S(1)}, bf16[16,4096]{1,0:T(8,128)(2,1)S(1)}, bf16[16,4096]{1,0:T(8,128)(2,1)S(1)}) custom-call(s32[32]{0:T(128)S(1)} %minimum_add_fusion.slots, bf16[64,128,128]{2,1,0:T(8,128)(2,1)S(1)} %bitcast.37), custom_call_target="tpu_custom_call" | custom-call | tf_op jit(solution)/shard_map/phases/pallas_call | solution.py:334
  44.3 3.8 %collective-permute-start = (bf16[16,4096]{1,0:T(8,128)(2,1)S(1)}, bf16[16,4096]{1,0:T(8,128)(2,1)S(1)}, u32[]{:S(2)}, u32[]{:S(2)}) collective-permute-start(bf16[16,4096]{1,0:T(8,128)(2,1)S(1)} %get-tuple-element.10), channel_id=1, source_target_pairs={{0,1},{1,2},{2,3},{3,4},{4,5},{5,6},{6,7},{8,9},{9,10},{10,11},{11... | collective-permute-start | bytes 393224 | tf_op jit(solution)/shard_map/ppermute | solution.py:344
  48.2 4.6 %collective-permute-start.1 = (bf16[16,4096]{1,0:T(8,128)(2,1)S(1)}, bf16[16,4096]{1,0:T(8,128)(2,1)S(1)}, u32[]{:S(2)}, u32[]{:S(2)}) collective-permute-start(bf16[16,4096]{1,0:T(8,128)(2,1)S(1)} %get-tuple-element.11), channel_id=1, source_target_pairs={{1,0},{2,1},{3,2},{4,3},{5,4},{6,5},{7,6},{9,8},{10,9},{11,10},{12... | collective-permute-start | bytes 393224 | tf_op jit(solution)/shard_map/ppermute | solution.py:345
  52.8 0.0 copy-done
  52.8 10.3 %main.1.partial = f32[128,4096]{1,0:T(8,128)} custom-call(bf16[2,128,2048]{2,1,0:T(8,128)(2,1)S(1)} %get-tuple-element.13.planes, bf16[2,384,1792]{2,1,0:T(8,128)(2,1)} %get-tuple-element.14.weights, f32[128,4096]{1,0:T(8,128)S(1)} %bitcast.38), custom_call_target="tpu_custom_call" | custom-call | flops 11000000512 | bytes 8000000 | tf_op jit(solution)/shard_map/main/pallas_call | solution.py:348
  63.1 0.0 collective-permute-done.above
  63.1 0.0 collective-permute-done.1.below
  63.1 2.9 %rim.1 = f32[128,4096]{1,0:T(8,128)} custom-call(s32[2]{0:T(128)S(1)} %add_convert_fusion.inner, bf16[16,4096]{1,0:T(8,128)(2,1)S(1)} %collective-permute-done.above, bf16[16,4096]{1,0:T(8,128)(2,1)S(1)} %collective-permute-done.1.below, bf16[2,96,384]{2,1,0:T(8,128)(2,1)S(1)} %get-tuple-element.12.weights, ...), custom_call_target="tpu_custom_call", output_to_operand_aliasing={{}: (4, {})} | custom-call | tf_op jit(solution)/shard_map/rim/pallas_call | solution.py:362
  (1 shorter events, 0.0 us)
Async XLA Ops:
  7.4 6.3 %copy-start.1 = (f32[40,2688]{1,0:T(8,128)S(1)}, f32[40,2688]{1,0:T(8,128)}, u32[]{:S(2)}) copy-start(f32[40,2688]{1,0:T(8,128)} %constant.28.clone) | copy-start | bytes 1290244
  7.4 6.3 %copy-start.2 = (f32[1,40,6]{1,0,2:T(1,128)S(1)}, f32[1,40,6]{1,0,2:T(1,128)}, u32[]{:S(2)}) copy-start(f32[1,40,6]{1,0,2:T(1,128)} %param.9) | copy-start | bytes 2884
  7.5 35.9 %all-to-all-start = ((bf16[16,512,128]{2,1,0:T(8,128)(2,1)}), bf16[16,512,128]{2,1,0:T(8,128)(2,1)S(1)}, u32[]{:S(2)}, u32[]{:S(2)}) async-start(bf16[16,512,128]{2,1,0:T(8,128)(2,1)} %bitcast.39), calls=%async_computation | async-start | bytes 4194304 | tf_op jit(solution)/shard_map/all_to_all | solution.py:313
  43.3 9.5 %copy-start = (f32[1,128,4096]{2,1,0:T(8,128)S(1)}, f32[1,128,4096]{2,1,0:T(8,128)}, u32[]{:S(2)}) copy-start(f32[1,128,4096]{2,1,0:T(8,128)} %param.7) | copy-start | bytes 6291460
  44.3 18.8 %collective-permute-start = (bf16[16,4096]{1,0:T(8,128)(2,1)S(1)}, bf16[16,4096]{1,0:T(8,128)(2,1)S(1)}, u32[]{:S(2)}, u32[]{:S(2)}) collective-permute-start(bf16[16,4096]{1,0:T(8,128)(2,1)S(1)} %get-tuple-element.10), channel_id=1, source_target_pairs={{0,1},{1,2},{2,3},{3,4},{4,5},{5,6},{6,7},{8,9},{9,10},{10,11},{11... | collective-permute-start | bytes 393224 | tf_op jit(solution)/shard_map/ppermute | solution.py:344
  48.2 15.0 %collective-permute-start.1 = (bf16[16,4096]{1,0:T(8,128)(2,1)S(1)}, bf16[16,4096]{1,0:T(8,128)(2,1)S(1)}, u32[]{:S(2)}, u32[]{:S(2)}) collective-permute-start(bf16[16,4096]{1,0:T(8,128)(2,1)S(1)} %get-tuple-element.11), channel_id=1, source_target_pairs={{1,0},{2,1},{3,2},{4,3},{5,4},{6,5},{7,6},{9,8},{10,9},{11,10},{12... | collective-permute-start | bytes 393224 | tf_op jit(solution)/shard_map/ppermute | solution.py:345

commit v2 on v1

--- a/solution.py
+++ b/solution.py
@@ -18,7 +18,7 @@
 SIDE = 64
 WIN = 80
 EDGE = 16
-K_MAIN = (TAPS + 1) * WIN
+K_MAIN = TAPS * WIN
 K_PAD = 1792
 K_EDGE = (TAPS + 1) * EDGE
 K_EDGE_PAD = 384
@@ -54,7 +54,8 @@
     return np.stack(rows)
 
 
-def cut_kernel(here, codes, patches, send, halves, listed, table, sems, table_sem):
+def cut_kernel(here, owners, numbers, offsets, patches, send, halves, *scratch):
+    near_owners, near_numbers, near_offsets, listed, table, sems, index_sems, table_sem = scratch
     step = pl.program_id(0)
 
     @pl.when(step == 0)
@@ -68,10 +69,20 @@
             for patch in range(4)
             for side in range(2)
         ]
-        for copy in copies:
+        indices = [
+            pltpu.make_async_copy(owners, near_owners, index_sems.at[0]),
+            pltpu.make_async_copy(numbers, near_numbers, index_sems.at[1]),
+            pltpu.make_async_copy(offsets, near_offsets, index_sems.at[2]),
+        ]
+        for copy in indices + copies:
             copy.start()
-        code = codes[here[0]]
-        mine = (code & 15) == here[1]
+        for copy in indices:
+            copy.wait()
+        strips = lambda array: array[:, pl.ds(here[0], 1), :].reshape(16, 32)
+        owner = strips(near_owners)
+        shift = near_offsets[:, pl.ds(here[0], 1)].reshape(16, 2, 32)
+        code = owner + strips(near_numbers) * 16 + shift[:, 0] * 64 + shift[:, 1] * 16384
+        mine = owner == here[1]
         earlier = lax.broadcasted_iota(jnp.int32, (32, 32), 0) < lax.broadcasted_iota(jnp.int32, (32, 32), 1)
         as_bf16 = lambda mask: mask.astype(jnp.float32).astype(jnp.bfloat16)
         rank = jnp.dot(as_bf16(mine), as_bf16(earlier), preferred_element_type=jnp.float32)
@@ -95,9 +106,10 @@
         at = ((code >> 4) & 3) * 512 + ((code >> 6) & 255)
         dx = (code >> 14) & 255
         turn = (TS - dx) & (TS - 1)
-        low = pltpu.roll(halves[pl.ds(at, TS), :], turn, 1)
-        high = pltpu.roll(halves[pl.ds(at + 256, TS), :], turn, 1)
-        send[slot] = jnp.where(lane < TS - dx, low, high).astype(jnp.bfloat16)
+        low = halves[pl.ds(at, TS), :]
+        high = halves[pl.ds(at + 256, TS), :]
+        mixed = jnp.where(lane >= dx, low, high).astype(jnp.bfloat16)
+        send[slot] = pltpu.roll(mixed, turn, 1)
         return carry
 
     lax.fori_loop(0, CUT, tile, 0, unroll=4)
@@ -143,7 +155,6 @@
                     at = slice(a * EDGE, (a + 1) * EDGE)
                     edge[half, at, group * 128 : (group + 1) * 128] = held_rim.astype(jnp.bfloat16)
                     held_rim = jnp.zeros((EDGE, 128), jnp.float32)
-        main[half, 3 * SIDE :, :] = pltpu.roll(main[half, : 3 * SIDE, :], WIN, 1)
         edge[half, 3 * EDGE :, :] = pltpu.roll(edge[half, : 3 * EDGE, :], EDGE, 1)
 
 
@@ -170,12 +181,23 @@
 
 def fold(parts, first, rows):
     folded = []
-    for phase in range(2):
-        x = 2 * (first + lax.broadcasted_iota(jnp.int32, (rows, parts.shape[1]), 1)) + phase
+    for phase, part in enumerate(parts):
+        x = 2 * (first + lax.broadcasted_iota(jnp.int32, (rows, part.shape[1]), 1)) + phase
         xh = (2.0 * x.astype(jnp.float32) + 1.0) / 4096.0 - 1.0
-        terms = [parts[(phase * 3 + a) * rows : (phase * 3 + a + 1) * rows] for a in range(3)]
+        terms = [part[a * rows : (a + 1) * rows] for a in range(3)]
         folded.append(terms[0] + xh * (terms[1] + xh * terms[2]))
     return folded
+
+
+def product(weights, lags):
+    return [
+        jnp.dot(
+            weights,
+            lags[phase : phase + TAPS].reshape(weights.shape[1], lags.shape[2]),
+            preferred_element_type=jnp.float32,
+        )
+        for phase in range(2)
+    ]
 
 
 def together(pieces, join):
@@ -196,20 +218,20 @@
     if lag == 0:
         return tiles[1:-1]
     lane = lax.broadcasted_iota(jnp.int32, tiles[0].shape, 1)
-    turned = [pltpu.roll(tile, (-lag) % TS, 1) for tile in tiles]
     if lag > 0:
-        return [jnp.where(lane < TS - lag, turned[i], turned[i + 1]) for i in range(1, len(tiles) - 1)]
-    return [jnp.where(lane < -lag, turned[i - 1], turned[i]) for i in range(1, len(tiles) - 1)]
+        mixed = [jnp.where(lane >= lag, tiles[i], tiles[i + 1]) for i in range(1, len(tiles) - 1)]
+    else:
+        mixed = [jnp.where(lane < TS + lag, tiles[i], tiles[i - 1]) for i in range(1, len(tiles) - 1)]
+    return [pltpu.roll(tile, (-lag) % TS, 1) for tile in mixed]
 
 
 def main_kernel(planes, weights, science, out, even, odd, held, sems):
     step = pl.program_id(0)
     copies = [
-        pltpu.make_async_copy(weights.at[half, pl.ds(part * 96, 96)], held.at[half, pl.ds(part * 96, 96)], sems.at[half, part])
+        pltpu.make_async_copy(weights.at[half, pl.ds(part * 48, 48)], held.at[half, pl.ds(part * 48, 48)], sems.at[half, part])
         for half in range(2)
         for part in range(4)
     ]
-
     def shift(first, buffer):
         near = []
         for phase in range(2):
@@ -227,8 +249,7 @@
     def multiply(first, buffer):
         pieces = []
         for half in range(2):
-            source = buffer[:, half * 48 : half * 48 + WIN, :].reshape(K_MAIN, WIDE)
-            parts = jnp.dot(held[half, :, :K_MAIN], source, preferred_element_type=jnp.float32)
+            parts = product(held[half, :, :K_MAIN], buffer[:, half * 48 : half * 48 + WIN, :])
             folded = fold(parts, first * TS, SIDE)
             pieces += [paired(folded, i) for i in range(TILES)]
         return pieces
@@ -272,6 +293,7 @@
         for first in range(0, 16, 4):
             lags = shifted[number, :, :, first * TS : (first + 4) * TS].reshape(K_EDGE, 4 * TS)
             parts = jnp.dot(weights[number, :, :K_EDGE], lags, preferred_element_type=jnp.float32)
+            parts = [parts[: 3 * EDGE], parts[3 * EDGE :]]
             folded = fold(parts, first * TS, EDGE)
             pieces += [paired(folded, i) for i in range(4)]
     models = together(pieces, apart(True))
@@ -288,28 +310,37 @@
 def per_device(science, patches, coeffs, tile_owner, tile_patch, tile_offset):
     ccd_id = lax.axis_index("ccd")
     amp_id = lax.axis_index("amp")
-    codes = tile_owner[..., 0] | (tile_patch << 4) | (tile_offset[..., 0] << 6) | (tile_offset[..., 1] << 14)
-    codes = codes.transpose(1, 0, 2)
     here = jnp.stack([amp_id, ccd_id])
 
+    far = lambda array: pltpu.with_memory_space_constraint(array, pltpu.HBM)
     whole = pl.BlockSpec(memory_space=pltpu.VMEM)
     scalars = pl.BlockSpec(memory_space=pltpu.SMEM)
     send = pl.pallas_call(
         cut_kernel,
         grid=(16 * CAP // CUT,),
         out_shape=pltpu.HBM((16 * CAP, TS, TS), jnp.bfloat16),
-        in_specs=[scalars, whole, pl.BlockSpec(memory_space=pl.ANY)],
+        in_specs=[scalars] + [pl.BlockSpec(memory_space=pl.ANY)] * 4,
         out_specs=pl.BlockSpec((CUT, TS, TS), lambda i: (i, 0, 0)),
         scratch_shapes=[
             pltpu.VMEM((4 * 2 * 256, TS), jnp.float32),
+            pltpu.VMEM((16, 8, 32), jnp.int32),
+            pltpu.VMEM((16, 8, 32), jnp.int32),
+            pltpu.VMEM((16, 8, 2, 32), jnp.int32),
             pltpu.VMEM((16, 128), jnp.int32),
             pltpu.SMEM((16, 128), jnp.int32),
             pltpu.SemaphoreType.DMA((4, 2)),
+            pltpu.SemaphoreType.DMA((3,)),
             pltpu.SemaphoreType.DMA,
         ],
         compiler_params=pltpu.CompilerParams(vmem_limit_bytes=10 * MIB),
         name="cut",
-    )(here, codes, pltpu.with_memory_space_constraint(patches.reshape(4, 256, 256), pltpu.HBM))
+    )(
+        here,
+        far(tile_owner.reshape(16, 8, 32)),
+        far(tile_patch),
+        far(tile_offset.transpose(0, 1, 3, 2)),
+        far(patches.reshape(4, 256, 256)),
+    )
     tiles = lax.all_to_all(send.reshape(16, CAP * TS, TS), "ccd", 0, 0, tiled=True).reshape(16 * CAP, TS, TS)
 
     order = jnp.arange(32)
@@ -321,7 +352,7 @@
     main, edge = pl.pallas_call(
         weights_kernel,
         out_shape=(
-            pltpu.HBM((2, 6 * SIDE, K_PAD), jnp.bfloat16),
+            pltpu.HBM((2, 3 * SIDE, K_PAD), jnp.bfloat16),
             jax.ShapeDtypeStruct((2, 6 * EDGE, K_EDGE_PAD), jnp.bfloat16),
         ),
         in_specs=[scalars, whole],
@@ -351,7 +382,7 @@
         in_specs=[whole, pl.BlockSpec(memory_space=pl.ANY), columns],
         out_specs=columns,
         scratch_shapes=[pltpu.VMEM((LAGS, ROWS, WIDE), jnp.bfloat16)] * 2
-        + [pltpu.VMEM((2, 6 * SIDE, K_PAD), jnp.bfloat16), pltpu.SemaphoreType.DMA((2, 4))],
+        + [pltpu.VMEM((2, 3 * SIDE, K_PAD), jnp.bfloat16), pltpu.SemaphoreType.DMA((2, 4))],
         out_shape=jax.ShapeDtypeStruct((ROWS, 4096), jnp.float32),
         compiler_params=pltpu.CompilerParams(vmem_limit_bytes=24 * MIB),
         cost_estimate=pl.CostEstimate(flops=11_000_000_000, bytes_accessed=8_000_000, transcendentals=0),

time: 66.4 us -> 64.6 us (0.973)
  waiting for transfers between devices: 7.42 us -> 9.12 us
  Pallas kernels: 39.7 us -> 38.3 us
  local copies, waits for them, and re-layouts: 1.77 us -> 0.67 us
  other arithmetic: 1.92 us -> 0.99 us
    all_to_all x1, waiting for transfers between devices: 7.42 us -> 9.11 us  [per_device(): lax.all_to_all(send.reshape(16, CAP * TS, TS), 'ccd', 0, 0, tiled=True)]
    pallas_call x1, Pallas kernels: 20.2 us -> 18.5 us  [per_device(): pl.pallas_call(weights_kernel, out_shape=(pltpu.HBM((2, 3 * SIDE, K_PAD),...]
    slice x1 -> x0, local copies, waits for them, and re-layouts: 1.09 us -> none  [per_device(): tile_offset[..., 0] << 6]
    transpose x1 -> x0, other arithmetic: 0.92 us -> none  [per_device(): codes = codes.transpose(1, 0, 2)]
  transfers between devices with their start and end apart: 3 -> 3, of which waited for: 1 -> 1; matrix products, arithmetic and copies ran while one was open for 3% -> 3% of each run, Pallas kernels for 46% -> 44%
where the time goes in v2:
time: 64.6 us; the launch traced here: 64.3 us
  Pallas kernels  38.3 us (59%)
  starting transfers between devices  14.7 us (23%)
  waiting for transfers between devices  9.12 us (14%)
  other arithmetic  0.99 us (2%)
  local copies, waits for them, and re-layouts  0.67 us (1%)
    pallas_call x1, Pallas kernels, per_device(): pl.pallas_call(weights_kernel, out_shape=(pltpu.HBM((2, 3 * SIDE, K_PAD),...  18.5 us
    pallas_call x1, Pallas kernels, per_device(): pl.pallas_call(main_kernel, grid=(4096 // (2 * BLOCK),), in_specs=[whole,...  10 us
    all_to_all x1, waiting for transfers between devices, per_device(): lax.all_to_all(send.reshape(16, CAP * TS, TS), 'ccd', 0, 0, tiled=True)  9.11 us
    all_to_all x1, starting transfers between devices, per_device(): lax.all_to_all(send.reshape(16, CAP * TS, TS), 'ccd', 0, 0, tiled=True)  6.28 us
    pallas_call x1, Pallas kernels, per_device(): pl.pallas_call(cut_kernel, grid=(16 * CAP // CUT,), out_shape=pltpu.HBM((...  5.92 us
    ppermute x1, starting transfers between devices, per_device(): below = lax.ppermute(top, 'amp', [(b, a) for a, b in down])  4.63 us
    ppermute x1, starting transfers between devices, per_device(): above = lax.ppermute(bottom, 'amp', down)  3.83 us
    pallas_call x1, Pallas kernels, per_device(): pl.pallas_call(rim_kernel, in_specs=[scalars, whole, whole, whole, pl.Blo...  2.89 us
  transfers between devices with their start and end apart: 3, of which 1 were waited for; matrix products, arithmetic and copies ran while one was open for 3% of the time, Pallas kernels for 44%

profile of v2, /device:TPU:2, one launch (start us, length us, event | category | flops | bytes accessed | tf_op | source)
XLA Modules:
  0.0 64.3 jit_solution(6316686117709180548)
XLA Ops:
  0.0 0.1 pad_add_fusion.here
  0.1 5.9 %cut.1 = bf16[64,128,128]{2,1,0:T(8,128)(2,1)} custom-call(s32[2]{0:T(128)S(1)} %pad_add_fusion.here, s32[16,8,32]{2,1,0:T(8,128)} %bitcast.26, s32[16,8,32]{2,1,0:T(8,128)} %numbers.1, s32[16,8,2,32]{3,2,1,0:T(2,128)} %bitcast.25, f32[4,256,256]{2,1,0:T(8,128)} %bitcast.24), custom_call_target="tpu_custom_call" | custom-call | tf_op jit(solution)/shard_map/cut/pallas_call | solution.py:318
  6.0 0.0 copy-start.1
  6.0 0.0 copy-start.2
  6.0 6.3 %all-to-all-start = ((bf16[16,512,128]{2,1,0:T(8,128)(2,1)}), bf16[16,512,128]{2,1,0:T(8,128)(2,1)S(1)}, u32[]{:S(2)}, u32[]{:S(2)}) async-start(bf16[16,512,128]{2,1,0:T(8,128)(2,1)} %bitcast.23), calls=%async_computation | async-start | bytes 4194304 | tf_op jit(solution)/shard_map/all_to_all | solution.py:344
  12.3 0.0 copy-done.1
  12.3 0.0 copy-done.2
  12.3 0.3 convolution_bitcast_fusion.moments
  12.7 18.5 %weights.1 = (bf16[2,192,1792]{2,1,0:T(8,128)(2,1)}, bf16[2,96,384]{2,1,0:T(8,128)(2,1)S(1)}) custom-call(s32[1]{0:T(128)} %bitcast.3.amp, f32[6,2688]{1,0:T(8,128)S(1)} %convolution_bitcast_fusion.moments), custom_call_target="tpu_custom_call" | custom-call | flops 50000000 | bytes 2000000 | tf_op jit(solution)/shard_map/weights/pallas_call | solution.py:352
  31.2 0.1 add_convert_fusion.inner
  31.3 0.7 %dynamic-slice_bitcast_fusion = s32[32]{0:T(128)S(1)} fusion(s32[16,8,32,1]{2,3,1,0:T(1,128)} %param.10, s32[]{:T(128)S(6)} %select_n.6, s32[]{:T(128)S(6)} %select_n.7), kind=kLoop, calls=%fused_computation.8 | loop fusion | bytes 264 | tf_op jit(solution)/shard_map/squeeze | solution.py:347
  31.9 0.2 convert_reduce_fusion
  32.1 0.7 %minimum_add_fusion.slots = s32[32]{0:T(128)S(1)} fusion(s32[32]{0:T(128)S(1)} %convert_reduce_fusion, s32[16,8,32,1]{2,3,1,0:T(1,128)} %param.10, s32[]{:T(128)S(6)} %select_n.6, s32[]{:T(128)S(6)} %select_n.7), kind=kLoop, calls=%fused_computation.7 | loop fusion | flops 96 | bytes 392 | tf_op jit(solution)/shard_map/add | solution.py:349
  32.8 9.1 %all-to-all-done = bf16[16,512,128]{2,1,0:T(8,128)(2,1)S(1)} async-done(((bf16[16,512,128]{2,1,0:T(8,128)(2,1)}), bf16[16,512,128]{2,1,0:T(8,128)(2,1)S(1)}, u32[]{:S(2)}, u32[]{:S(2)}) %all-to-all-start) | async-done | bytes 2097184 | tf_op jit(solution)/shard_map/all_to_all | solution.py:344
  41.9 0.0 copy-start
  41.9 1.0 %phases.1 = (bf16[2,128,2048]{2,1,0:T(8,128)(2,1)S(1)}, bf16[16,4096]{1,0:T(8,128)(2,1)S(1)}, bf16[16,4096]{1,0:T(8,128)(2,1)S(1)}) custom-call(s32[32]{0:T(128)S(1)} %minimum_add_fusion.slots, bf16[64,128,128]{2,1,0:T(8,128)(2,1)S(1)} %bitcast.21), custom_call_target="tpu_custom_call" | custom-call | tf_op jit(solution)/shard_map/phases/pallas_call | solution.py:365
  42.9 3.8 %collective-permute-start = (bf16[16,4096]{1,0:T(8,128)(2,1)S(1)}, bf16[16,4096]{1,0:T(8,128)(2,1)S(1)}, u32[]{:S(2)}, u32[]{:S(2)}) collective-permute-start(bf16[16,4096]{1,0:T(8,128)(2,1)S(1)} %get-tuple-element.10), channel_id=1, source_target_pairs={{0,1},{1,2},{2,3},{3,4},{4,5},{5,6},{6,7},{8,9},{9,10},{10,11},{11... | collective-permute-start | bytes 393224 | tf_op jit(solution)/shard_map/ppermute | solution.py:375
  46.7 4.6 %collective-permute-start.1 = (bf16[16,4096]{1,0:T(8,128)(2,1)S(1)}, bf16[16,4096]{1,0:T(8,128)(2,1)S(1)}, u32[]{:S(2)}, u32[]{:S(2)}) collective-permute-start(bf16[16,4096]{1,0:T(8,128)(2,1)S(1)} %get-tuple-element.11), channel_id=1, source_target_pairs={{1,0},{2,1},{3,2},{4,3},{5,4},{6,5},{7,6},{9,8},{10,9},{11,10},{12... | collective-permute-start | bytes 393224 | tf_op jit(solution)/shard_map/ppermute | solution.py:376
  51.4 0.0 copy-done
  51.4 10.0 %main.1.partial = f32[128,4096]{1,0:T(8,128)} custom-call(bf16[2,128,2048]{2,1,0:T(8,128)(2,1)S(1)} %get-tuple-element.13.planes, bf16[2,192,1792]{2,1,0:T(8,128)(2,1)} %get-tuple-element.14.weights, f32[128,4096]{1,0:T(8,128)S(1)} %bitcast.22), custom_call_target="tpu_custom_call" | custom-call | flops 11000000512 | bytes 8000000 | tf_op jit(solution)/shard_map/main/pallas_call | solution.py:379
  61.4 0.0 collective-permute-done.above
  61.4 0.0 collective-permute-done.1.below
  61.4 2.9 %rim.1 = f32[128,4096]{1,0:T(8,128)} custom-call(s32[2]{0:T(128)S(1)} %add_convert_fusion.inner, bf16[16,4096]{1,0:T(8,128)(2,1)S(1)} %collective-permute-done.above, bf16[16,4096]{1,0:T(8,128)(2,1)S(1)} %collective-permute-done.1.below, bf16[2,96,384]{2,1,0:T(8,128)(2,1)S(1)} %get-tuple-element.12.weights, ...), custom_call_target="tpu_custom_call", output_to_operand_aliasing={{}: (4, {})} | custom-call | tf_op jit(solution)/shard_map/rim/pallas_call | solution.py:393
Async XLA Ops:
  6.0 6.3 %copy-start.1 = (f32[40,2688]{1,0:T(8,128)S(1)}, f32[40,2688]{1,0:T(8,128)}, u32[]{:S(2)}) copy-start(f32[40,2688]{1,0:T(8,128)} %constant.23.clone) | copy-start | bytes 1290244
  6.0 6.3 %copy-start.2 = (f32[1,40,6]{1,0,2:T(1,128)S(1)}, f32[1,40,6]{1,0,2:T(1,128)}, u32[]{:S(2)}) copy-start(f32[1,40,6]{1,0,2:T(1,128)} %param.9) | copy-start | bytes 2884
  6.0 35.9 %all-to-all-start = ((bf16[16,512,128]{2,1,0:T(8,128)(2,1)}), bf16[16,512,128]{2,1,0:T(8,128)(2,1)S(1)}, u32[]{:S(2)}, u32[]{:S(2)}) async-start(bf16[16,512,128]{2,1,0:T(8,128)(2,1)} %bitcast.23), calls=%async_computation | async-start | bytes 4194304 | tf_op jit(solution)/shard_map/all_to_all | solution.py:344
  41.9 9.5 %copy-start = (f32[1,128,4096]{2,1,0:T(8,128)S(1)}, f32[1,128,4096]{2,1,0:T(8,128)}, u32[]{:S(2)}) copy-start(f32[1,128,4096]{2,1,0:T(8,128)} %param.7) | copy-start | bytes 6291460
  42.9 18.5 %collective-permute-start = (bf16[16,4096]{1,0:T(8,128)(2,1)S(1)}, bf16[16,4096]{1,0:T(8,128)(2,1)S(1)}, u32[]{:S(2)}, u32[]{:S(2)}) collective-permute-start(bf16[16,4096]{1,0:T(8,128)(2,1)S(1)} %get-tuple-element.10), channel_id=1, source_target_pairs={{0,1},{1,2},{2,3},{3,4},{4,5},{5,6},{6,7},{8,9},{9,10},{10,11},{11... | collective-permute-start | bytes 393224 | tf_op jit(solution)/shard_map/ppermute | solution.py:375
  46.7 14.7 %collective-permute-start.1 = (bf16[16,4096]{1,0:T(8,128)(2,1)S(1)}, bf16[16,4096]{1,0:T(8,128)(2,1)S(1)}, u32[]{:S(2)}, u32[]{:S(2)}) collective-permute-start(bf16[16,4096]{1,0:T(8,128)(2,1)S(1)} %get-tuple-element.11), channel_id=1, source_target_pairs={{1,0},{2,1},{3,2},{4,3},{5,4},{6,5},{7,6},{9,8},{10,9},{11,10},{12... | collective-permute-start | bytes 393224 | tf_op jit(solution)/shard_map/ppermute | solution.py:376

commit v3 on v2

--- a/solution.py
+++ b/solution.py
@@ -26,7 +26,7 @@
 WIDE = BLOCK // 2
 TILES = WIDE // TS
 LAGS = TAPS + 1
-CUT = 16
+CUT = 32
 MIB = 1 << 20
 
 
@@ -112,10 +112,11 @@
         send[slot] = pltpu.roll(mixed, turn, 1)
         return carry
 
-    lax.fori_loop(0, CUT, tile, 0, unroll=4)
-
-
-def weights_kernel(amp, moments, main, edge):
+    lax.fori_loop(0, CUT, tile, 0, unroll=CUT)
+
+
+def weights_kernel(amp, moments, *outs):
+    main, edge = outs[:6], outs[6]
     first_row = amp[0] * ROWS
     lane = lax.broadcasted_iota(jnp.int32, (SIDE, 128), 1)
     lane16 = lax.broadcasted_iota(jnp.int32, (EDGE, 128), 1)
@@ -142,12 +143,11 @@
                 end = low + WIN
                 turned = across(pltpu.roll(moment, (lead + low) % 128, 1), members, yh)
                 held = jnp.where((lane >= low) & (lane < end), turned, held)
-                at = slice(a * SIDE, (a + 1) * SIDE)
                 if end >= 128 or last:
-                    main[half, at, group * 128 : (group + 1) * 128] = held.astype(jnp.bfloat16)
+                    main[half * 3 + a][:, group * 128 : (group + 1) * 128] = held.astype(jnp.bfloat16)
                     held = jnp.where(lane < end - 128, turned, 0.0)
                     if last and end > 128:
-                        main[half, at, (group + 1) * 128 : (group + 2) * 128] = held.astype(jnp.bfloat16)
+                        main[half * 3 + a][:, (group + 1) * 128 : (group + 2) * 128] = held.astype(jnp.bfloat16)
                 group, low = u * EDGE // 128, u * EDGE % 128
                 turned = across(pltpu.roll(moment, (rim_lead + low) % 128, 1), members, yh[rim])
                 held_rim = jnp.where((lane16 >= low) & (lane16 < low + EDGE), turned, held_rim)
@@ -166,7 +166,9 @@
     return (column == home).astype(jnp.float32).astype(jnp.bfloat16)
 
 
-def phase_kernel(slots, tiles, planes, top, bottom):
+def phase_kernel(slots, tiles, far_weights, planes, top, bottom, near_weights, sem):
+    copy = pltpu.make_async_copy(far_weights, near_weights, sem)
+    copy.start()
     split = apart(False)
     for pair in range(16):
         both = jnp.concatenate([tiles[slots[2 * pair]], tiles[slots[2 * pair + 1]]], axis=1)
@@ -177,6 +179,7 @@
             at = slice(phase * 2048 + pair * TS, phase * 2048 + (pair + 1) * TS)
             top[:, at] = piece[:EDGE]
             bottom[:, at] = piece[TS - EDGE :]
+    copy.wait()
 
 
 def fold(parts, first, rows):
@@ -225,13 +228,10 @@
     return [pltpu.roll(tile, (-lag) % TS, 1) for tile in mixed]
 
 
-def main_kernel(planes, weights, science, out, even, odd, held, sems):
+def main_kernel(planes, *refs):
+    weights, (science, out, even, odd) = refs[:6], refs[6:]
     step = pl.program_id(0)
-    copies = [
-        pltpu.make_async_copy(weights.at[half, pl.ds(part * 48, 48)], held.at[half, pl.ds(part * 48, 48)], sems.at[half, part])
-        for half in range(2)
-        for part in range(4)
-    ]
+
     def shift(first, buffer):
         near = []
         for phase in range(2):
@@ -249,18 +249,15 @@
     def multiply(first, buffer):
         pieces = []
         for half in range(2):
-            parts = product(held[half, :, :K_MAIN], buffer[:, half * 48 : half * 48 + WIN, :])
+            members = [weights[half * 3 + a][:, :K_MAIN] for a in range(3)]
+            parts = product(jnp.concatenate(members, axis=0), buffer[:, half * 48 : half * 48 + WIN, :])
             folded = fold(parts, first * TS, SIDE)
             pieces += [paired(folded, i) for i in range(TILES)]
         return pieces
 
     @pl.when(step == 0)
     def _():
-        for copy in copies:
-            copy.start()
         shift(0, even)
-        for copy in copies:
-            copy.wait()
 
     first = step * 2 * TILES
     shift(first + TILES, odd)
@@ -349,28 +346,33 @@
     slots = mine * CAP + jnp.minimum(jnp.sum(earlier.astype(jnp.int32), axis=1), CAP - 1)
 
     moments = jnp.einsum("km,kl->ml", coeffs[0], jnp.asarray(basis_table()), precision=lax.Precision.HIGHEST)
-    main, edge = pl.pallas_call(
+    *main, edge = pl.pallas_call(
         weights_kernel,
         out_shape=(
-            pltpu.HBM((2, 3 * SIDE, K_PAD), jnp.bfloat16),
+            *([jax.ShapeDtypeStruct((SIDE, K_PAD), jnp.bfloat16)] * 5),
+            pltpu.HBM((SIDE, K_PAD), jnp.bfloat16),
             jax.ShapeDtypeStruct((2, 6 * EDGE, K_EDGE_PAD), jnp.bfloat16),
         ),
         in_specs=[scalars, whole],
-        out_specs=(whole, whole),
+        out_specs=(whole,) * 7,
         compiler_params=pltpu.CompilerParams(vmem_limit_bytes=10 * MIB),
         cost_estimate=pl.CostEstimate(flops=50_000_000, bytes_accessed=2_000_000, transcendentals=0),
         name="weights",
     )(amp_id.reshape(1), moments)
 
-    planes, top, bottom = pl.pallas_call(
+    planes, top, bottom, main[5] = pl.pallas_call(
         phase_kernel,
-        out_shape=(jax.ShapeDtypeStruct((2, ROWS, 2048), jnp.bfloat16),)
-        + (jax.ShapeDtypeStruct((EDGE, 4096), jnp.bfloat16),) * 2,
-        in_specs=[scalars, whole],
-        out_specs=(whole, whole, whole),
+        out_shape=(
+            jax.ShapeDtypeStruct((2, ROWS, 2048), jnp.bfloat16),
+            *([jax.ShapeDtypeStruct((EDGE, 4096), jnp.bfloat16)] * 2),
+            jax.ShapeDtypeStruct((SIDE, K_PAD), jnp.bfloat16),
+        ),
+        in_specs=[scalars, whole, pl.BlockSpec(memory_space=pl.ANY)],
+        out_specs=(whole,) * 4,
+        scratch_shapes=[pltpu.SemaphoreType.DMA],
         compiler_params=pltpu.CompilerParams(vmem_limit_bytes=8 * MIB),
         name="phases",
-    )(slots, tiles)
+    )(slots, tiles, far(main[5]))
     down = [(i, i + 1) for i in range(7)]
     above = lax.ppermute(bottom, "amp", down)
     below = lax.ppermute(top, "amp", [(b, a) for a, b in down])
@@ -379,15 +381,14 @@
     partial = pl.pallas_call(
         main_kernel,
         grid=(4096 // (2 * BLOCK),),
-        in_specs=[whole, pl.BlockSpec(memory_space=pl.ANY), columns],
+        in_specs=[whole] * 7 + [columns],
         out_specs=columns,
-        scratch_shapes=[pltpu.VMEM((LAGS, ROWS, WIDE), jnp.bfloat16)] * 2
-        + [pltpu.VMEM((2, 3 * SIDE, K_PAD), jnp.bfloat16), pltpu.SemaphoreType.DMA((2, 4))],
+        scratch_shapes=[pltpu.VMEM((LAGS, ROWS, WIDE), jnp.bfloat16)] * 2,
         out_shape=jax.ShapeDtypeStruct((ROWS, 4096), jnp.float32),
-        compiler_params=pltpu.CompilerParams(vmem_limit_bytes=24 * MIB),
+        compiler_params=pltpu.CompilerParams(vmem_limit_bytes=12 * MIB),
         cost_estimate=pl.CostEstimate(flops=11_000_000_000, bytes_accessed=8_000_000, transcendentals=0),
         name="main",
-    )(planes, pltpu.with_memory_space_constraint(main, pltpu.HBM), science[0])
+    )(planes, *main, science[0])
 
     inner = jnp.stack([amp_id > 0, amp_id < 7]).astype(jnp.int32)
     result = pl.pallas_call(
@@ -401,7 +402,7 @@
         ],
         out_shape=jax.ShapeDtypeStruct((ROWS, 4096), jnp.float32),
         input_output_aliases={4: 0},
-        compiler_params=pltpu.CompilerParams(vmem_limit_bytes=16 * MIB),
+        compiler_params=pltpu.CompilerParams(vmem_limit_bytes=10 * MIB),
         name="rim",
     )(inner, above, below, edge, partial)
     return result[None]

time: 64.6 us -> 62.7 us (0.971)
  Pallas kernels: 38.3 us -> 36.1 us
    pallas_call x2, Pallas kernels: 28.5 us -> 26.9 us  [the longest x1 18.1 us: per_device(): pl.pallas_call(weights_kernel, out_shape=(*[jax.ShapeDtypeStruct((SIDE, K...]
    pallas_call x1, Pallas kernels: 5.92 us -> 4.55 us  [per_device(): pl.pallas_call(cut_kernel, grid=(16 * CAP // CUT,), out_shape=pltpu.HBM((...]
    pallas_call x1, Pallas kernels: 0.99 us -> 1.72 us  [per_device(): pl.pallas_call(phase_kernel, out_shape=(jax.ShapeDtypeStruct((2, ROWS, 20...]
  transfers between devices with their start and end apart: 3 -> 3, of which waited for: 1 -> 1; matrix products, arithmetic and copies ran while one was open for 3% -> 3% of each run, Pallas kernels for 44% -> 43%
where the time goes in v3:
time: 62.7 us; the launch traced here: 62.5 us
  Pallas kernels  36.1 us (58%)
  starting transfers between devices  14.7 us (23%)
  waiting for transfers between devices  9.55 us (15%)
  other arithmetic  0.99 us (2%)
  local copies, waits for them, and re-layouts  0.67 us (1%)
    pallas_call x1, Pallas kernels, per_device(): pl.pallas_call(weights_kernel, out_shape=(*[jax.ShapeDtypeStruct((SIDE, K...  18.1 us
    all_to_all x1, waiting for transfers between devices, per_device(): lax.all_to_all(send.reshape(16, CAP * TS, TS), 'ccd', 0, 0, tiled=True)  9.55 us
    pallas_call x1, Pallas kernels, per_device(): pl.pallas_call(main_kernel, grid=(4096 // (2 * BLOCK),), in_specs=[whole]...  8.84 us
    all_to_all x1, starting transfers between devices, per_device(): lax.all_to_all(send.reshape(16, CAP * TS, TS), 'ccd', 0, 0, tiled=True)  6.28 us
    ppermute x1, starting transfers between devices, per_device(): below = lax.ppermute(top, 'amp', [(b, a) for a, b in down])  4.63 us
    pallas_call x1, Pallas kernels, per_device(): pl.pallas_call(cut_kernel, grid=(16 * CAP // CUT,), out_shape=pltpu.HBM((...  4.55 us
    ppermute x1, starting transfers between devices, per_device(): above = lax.ppermute(bottom, 'amp', down)  3.83 us
    pallas_call x1, Pallas kernels, per_device(): pl.pallas_call(rim_kernel, in_specs=[scalars, whole, whole, whole, pl.Blo...  2.89 us
  transfers between devices with their start and end apart: 3, of which 1 were waited for; matrix products, arithmetic and copies ran while one was open for 3% of the time, Pallas kernels for 43%

profile of v3, /device:TPU:2, one launch (start us, length us, event | category | flops | bytes accessed | tf_op | source)
XLA Modules:
  0.0 62.5 jit_solution(6263391366809449419)
XLA Ops:
  0.0 0.1 pad_add_fusion.here
  0.1 4.6 %cut.1 = bf16[64,128,128]{2,1,0:T(8,128)(2,1)} custom-call(s32[2]{0:T(128)S(1)} %pad_add_fusion.here, s32[16,8,32]{2,1,0:T(8,128)} %bitcast.26, s32[16,8,32]{2,1,0:T(8,128)} %numbers.1, s32[16,8,2,32]{3,2,1,0:T(2,128)} %bitcast.25, f32[4,256,256]{2,1,0:T(8,128)} %bitcast.24), custom_call_target="tpu_custom_call" | custom-call | tf_op jit(solution)/shard_map/cut/pallas_call | solution.py:315
  4.6 0.0 copy-start.1
  4.7 0.0 copy-start.2
  4.7 6.3 %all-to-all-start = ((bf16[16,512,128]{2,1,0:T(8,128)(2,1)}), bf16[16,512,128]{2,1,0:T(8,128)(2,1)S(1)}, u32[]{:S(2)}, u32[]{:S(2)}) async-start(bf16[16,512,128]{2,1,0:T(8,128)(2,1)} %bitcast.23), calls=%async_computation | async-start | bytes 4194304 | tf_op jit(solution)/shard_map/all_to_all | solution.py:341
  11.0 0.0 copy-done.1
  11.0 0.0 copy-done.2
  11.0 0.3 convolution_bitcast_fusion.moments
  11.3 18.1 %weights.1 = (bf16[64,1792]{1,0:T(8,128)(2,1)S(1)}, bf16[64,1792]{1,0:T(8,128)(2,1)S(1)}, bf16[64,1792]{1,0:T(8,128)(2,1)S(1)}, bf16[64,1792]{1,0:T(8,128)(2,1)S...) custom-call(s32[1]{0:T(128)} %bitcast.3.amp, ...), custom_call_target="tpu_custom_call" | custom-call | flops 50000000 | bytes 2000000 | tf_op jit(solution)/shard_map/weights/pallas_call | solution.py:349
  29.4 0.1 add_convert_fusion.inner
  29.5 0.7 %dynamic-slice_bitcast_fusion = s32[32]{0:T(128)S(1)} fusion(s32[16,8,32,1]{2,3,1,0:T(1,128)} %param.10, s32[]{:T(128)S(6)} %select_n.6, s32[]{:T(128)S(6)} %select_n.7), kind=kLoop, calls=%fused_computation.8 | loop fusion | bytes 264 | tf_op jit(solution)/shard_map/squeeze | solution.py:344
  30.1 0.2 convert_reduce_fusion
  30.3 0.7 %minimum_add_fusion.slots = s32[32]{0:T(128)S(1)} fusion(s32[32]{0:T(128)S(1)} %convert_reduce_fusion, s32[16,8,32,1]{2,3,1,0:T(1,128)} %param.10, s32[]{:T(128)S(6)} %select_n.6, s32[]{:T(128)S(6)} %select_n.7), kind=kLoop, calls=%fused_computation.7 | loop fusion | flops 96 | bytes 392 | tf_op jit(solution)/shard_map/add | solution.py:346
  31.0 9.5 %all-to-all-done = bf16[16,512,128]{2,1,0:T(8,128)(2,1)S(1)} async-done(((bf16[16,512,128]{2,1,0:T(8,128)(2,1)}), bf16[16,512,128]{2,1,0:T(8,128)(2,1)S(1)}, u32[]{:S(2)}, u32[]{:S(2)}) %all-to-all-start) | async-done | bytes 2097184 | tf_op jit(solution)/shard_map/all_to_all | solution.py:341
  40.5 0.0 copy-start
  40.5 1.7 %phases.1 = (bf16[2,128,2048]{2,1,0:T(8,128)(2,1)S(1)}, bf16[16,4096]{1,0:T(8,128)(2,1)S(1)}, bf16[16,4096]{1,0:T(8,128)(2,1)S(1)}, bf16[64,1792]{1,0:T(8,128)(2,1)S(1)}) custom-call(s32[32]{0:T(128)S(1)} %minimum_add_fusion.slots, bf16[64,128,128]{2,1,0:T(8,128)(2,1)S(1)} %bitcast.21, bf16[64,1792]{1,0:T(8,128)(2,1)} %get-tuple-element.16.far_weights), custom_call_target="tpu_custom_call" | custom-call | tf_op jit(solution)/shard_map/phases/pallas_call | solution.py:363
  42.3 3.8 %collective-permute-start = (bf16[16,4096]{1,0:T(8,128)(2,1)S(1)}, bf16[16,4096]{1,0:T(8,128)(2,1)S(1)}, u32[]{:S(2)}, u32[]{:S(2)}) collective-permute-start(bf16[16,4096]{1,0:T(8,128)(2,1)S(1)} %get-tuple-element.17), channel_id=1, source_target_pairs={{0,1},{1,2},{2,3},{3,4},{4,5},{5,6},{6,7},{8,9},{9,10},{10,11},{11... | collective-permute-start | bytes 393224 | tf_op jit(solution)/shard_map/ppermute | solution.py:377
  46.1 4.6 %collective-permute-start.1 = (bf16[16,4096]{1,0:T(8,128)(2,1)S(1)}, bf16[16,4096]{1,0:T(8,128)(2,1)S(1)}, u32[]{:S(2)}, u32[]{:S(2)}) collective-permute-start(bf16[16,4096]{1,0:T(8,128)(2,1)S(1)} %get-tuple-element.18), channel_id=1, source_target_pairs={{1,0},{2,1},{3,2},{4,3},{5,4},{6,5},{7,6},{9,8},{10,9},{11,10},{12... | collective-permute-start | bytes 393224 | tf_op jit(solution)/shard_map/ppermute | solution.py:378
  50.7 0.0 copy-done
  50.7 8.8 %main.1.partial = f32[128,4096]{1,0:T(8,128)} custom-call(bf16[2,128,2048]{2,1,0:T(8,128)(2,1)S(1)} %get-tuple-element.20.planes, bf16[64,1792]{1,0:T(8,128)(2,1)S(1)} %get-tuple-element.21.refs_0_, bf16[64,1792]{1,0:T(8,128)(2,1)S(1)} %get-tuple-element.22.refs_1_, bf16[64,1792]{1,0:T(8,128)(2,1)S(1)} %get-tuple-element.23.refs_2_, ...), custom_call_target="tpu_custom_call" | custom-call | flops 11000000512 | bytes 8000000 | tf_op jit(solution)/shard_map/main/pallas_call | solution.py:381
  59.6 0.0 collective-permute-done.above
  59.6 0.0 collective-permute-done.1.below
  59.6 2.9 %rim.1 = f32[128,4096]{1,0:T(8,128)} custom-call(s32[2]{0:T(128)S(1)} %add_convert_fusion.inner, bf16[16,4096]{1,0:T(8,128)(2,1)S(1)} %collective-permute-done.above, bf16[16,4096]{1,0:T(8,128)(2,1)S(1)} %collective-permute-done.1.below, bf16[2,96,384]{2,1,0:T(8,128)(2,1)S(1)} %get-tuple-element.19.weights, ...), custom_call_target="tpu_custom_call", output_to_operand_aliasing={{}: (4, {})} | custom-call | tf_op jit(solution)/shard_map/rim/pallas_call | solution.py:394
Async XLA Ops:
  4.6 6.3 %copy-start.1 = (f32[40,2688]{1,0:T(8,128)S(1)}, f32[40,2688]{1,0:T(8,128)}, u32[]{:S(2)}) copy-start(f32[40,2688]{1,0:T(8,128)} %constant.23.clone) | copy-start | bytes 1290244
  4.7 6.3 %copy-start.2 = (f32[1,40,6]{1,0,2:T(1,128)S(1)}, f32[1,40,6]{1,0,2:T(1,128)}, u32[]{:S(2)}) copy-start(f32[1,40,6]{1,0,2:T(1,128)} %param.9) | copy-start | bytes 2884
  4.7 35.9 %all-to-all-start = ((bf16[16,512,128]{2,1,0:T(8,128)(2,1)}), bf16[16,512,128]{2,1,0:T(8,128)(2,1)S(1)}, u32[]{:S(2)}, u32[]{:S(2)}) async-start(bf16[16,512,128]{2,1,0:T(8,128)(2,1)} %bitcast.23), calls=%async_computation | async-start | bytes 4194304 | tf_op jit(solution)/shard_map/all_to_all | solution.py:341
  40.5 10.2 %copy-start = (f32[1,128,4096]{2,1,0:T(8,128)S(1)}, f32[1,128,4096]{2,1,0:T(8,128)}, u32[]{:S(2)}) copy-start(f32[1,128,4096]{2,1,0:T(8,128)} %param.7) | copy-start | bytes 6291460
  42.3 17.3 %collective-permute-start = (bf16[16,4096]{1,0:T(8,128)(2,1)S(1)}, bf16[16,4096]{1,0:T(8,128)(2,1)S(1)}, u32[]{:S(2)}, u32[]{:S(2)}) collective-permute-start(bf16[16,4096]{1,0:T(8,128)(2,1)S(1)} %get-tuple-element.17), channel_id=1, source_target_pairs={{0,1},{1,2},{2,3},{3,4},{4,5},{5,6},{6,7},{8,9},{9,10},{10,11},{11... | collective-permute-start | bytes 393224 | tf_op jit(solution)/shard_map/ppermute | solution.py:377
  46.1 13.5 %collective-permute-start.1 = (bf16[16,4096]{1,0:T(8,128)(2,1)S(1)}, bf16[16,4096]{1,0:T(8,128)(2,1)S(1)}, u32[]{:S(2)}, u32[]{:S(2)}) collective-permute-start(bf16[16,4096]{1,0:T(8,128)(2,1)S(1)} %get-tuple-element.18), channel_id=1, source_target_pairs={{1,0},{2,1},{3,2},{4,3},{5,4},{6,5},{7,6},{9,8},{10,9},{11,10},{12... | collective-permute-start | bytes 393224 | tf_op jit(solution)/shard_map/ppermute | solution.py:378

commit v4 on v3

--- a/solution.py
+++ b/solution.py
@@ -373,7 +373,7 @@
         compiler_params=pltpu.CompilerParams(vmem_limit_bytes=8 * MIB),
         name="phases",
     )(slots, tiles, far(main[5]))
-    down = [(i, i + 1) for i in range(7)]
+    down = [(i, (i + 1) % 8) for i in range(8)]
     above = lax.ppermute(bottom, "amp", down)
     below = lax.ppermute(top, "amp", [(b, a) for a, b in down])
 

time: 62.7 us -> 59.6 us (0.951); the launches traced: 62.5 us -> 58.7 us
  starting transfers between devices: 14.7 us -> 11.1 us
    ppermute x1, starting transfers between devices: 3.83 us -> 1.99 us  [per_device(): above = lax.ppermute(bottom, 'amp', down)]
    ppermute x1, starting transfers between devices: 4.63 us -> 2.8 us  [per_device(): below = lax.ppermute(top, 'amp', [(b, a) for a, b in down])]
  transfers between devices with their start and end apart: 3 -> 3, of which waited for: 1 -> 1; matrix products, arithmetic and copies ran while one was open for 3% -> 3% of each run, Pallas kernels for 43% -> 46%
where the time goes in v4:
time: 59.6 us; the launch traced here: 58.7 us
  Pallas kernels  36 us (60%)
  starting transfers between devices  11.1 us (19%)
  waiting for transfers between devices  9.55 us (16%)
  other arithmetic  0.99 us (2%)
  local copies, waits for them, and re-layouts  0.67 us (1%)
    pallas_call x1, Pallas kernels, per_device(): pl.pallas_call(weights_kernel, out_shape=(*[jax.ShapeDtypeStruct((SIDE, K...  18.1 us
    all_to_all x1, waiting for transfers between devices, per_device(): lax.all_to_all(send.reshape(16, CAP * TS, TS), 'ccd', 0, 0, tiled=True)  9.55 us
    pallas_call x1, Pallas kernels, per_device(): pl.pallas_call(main_kernel, grid=(4096 // (2 * BLOCK),), in_specs=[whole]...  8.81 us
    all_to_all x1, starting transfers between devices, per_device(): lax.all_to_all(send.reshape(16, CAP * TS, TS), 'ccd', 0, 0, tiled=True)  6.28 us
    pallas_call x1, Pallas kernels, per_device(): pl.pallas_call(cut_kernel, grid=(16 * CAP // CUT,), out_shape=pltpu.HBM((...  4.55 us
    pallas_call x1, Pallas kernels, per_device(): pl.pallas_call(rim_kernel, in_specs=[scalars, whole, whole, whole, pl.Blo...  2.89 us
    ppermute x1, starting transfers between devices, per_device(): below = lax.ppermute(top, 'amp', [(b, a) for a, b in down])  2.8 us
    ppermute x1, starting transfers between devices, per_device(): above = lax.ppermute(bottom, 'amp', down)  1.99 us
  transfers between devices with their start and end apart: 3, of which 1 were waited for; matrix products, arithmetic and copies ran while one was open for 3% of the time, Pallas kernels for 46%

profile of v4, /device:TPU:2, one launch (start us, length us, event | category | flops | bytes accessed | tf_op | source)
XLA Modules:
  0.0 58.7 jit_solution(2390400164360063905)
XLA Ops:
  0.0 0.1 pad_add_fusion.here
  0.1 4.6 %cut.1 = bf16[64,128,128]{2,1,0:T(8,128)(2,1)} custom-call(s32[2]{0:T(128)S(1)} %pad_add_fusion.here, s32[16,8,32]{2,1,0:T(8,128)} %bitcast.26, s32[16,8,32]{2,1,0:T(8,128)} %numbers.1, s32[16,8,2,32]{3,2,1,0:T(2,128)} %bitcast.25, f32[4,256,256]{2,1,0:T(8,128)} %bitcast.24), custom_call_target="tpu_custom_call" | custom-call | tf_op jit(solution)/shard_map/cut/pallas_call | solution.py:315
  4.6 0.0 copy-start.1
  4.6 0.0 copy-start.2
  4.7 6.3 %all-to-all-start = ((bf16[16,512,128]{2,1,0:T(8,128)(2,1)}), bf16[16,512,128]{2,1,0:T(8,128)(2,1)S(1)}, u32[]{:S(2)}, u32[]{:S(2)}) async-start(bf16[16,512,128]{2,1,0:T(8,128)(2,1)} %bitcast.23), calls=%async_computation | async-start | bytes 4194304 | tf_op jit(solution)/shard_map/all_to_all | solution.py:341
  11.0 0.0 copy-done.1
  11.0 0.0 copy-done.2
  11.0 0.3 convolution_bitcast_fusion.moments
  11.3 18.1 %weights.1 = (bf16[64,1792]{1,0:T(8,128)(2,1)S(1)}, bf16[64,1792]{1,0:T(8,128)(2,1)S(1)}, bf16[64,1792]{1,0:T(8,128)(2,1)S(1)}, bf16[64,1792]{1,0:T(8,128)(2,1)S...) custom-call(s32[1]{0:T(128)} %bitcast.3.amp, ...), custom_call_target="tpu_custom_call" | custom-call | flops 50000000 | bytes 2000000 | tf_op jit(solution)/shard_map/weights/pallas_call | solution.py:349
  29.4 0.1 add_convert_fusion.inner
  29.5 0.7 %dynamic-slice_bitcast_fusion = s32[32]{0:T(128)S(1)} fusion(s32[16,8,32,1]{2,3,1,0:T(1,128)} %param.10, s32[]{:T(128)S(6)} %select_n.6, s32[]{:T(128)S(6)} %select_n.7), kind=kLoop, calls=%fused_computation.8 | loop fusion | bytes 264 | tf_op jit(solution)/shard_map/squeeze | solution.py:344
  30.1 0.2 convert_reduce_fusion
  30.3 0.7 %minimum_add_fusion.slots = s32[32]{0:T(128)S(1)} fusion(s32[32]{0:T(128)S(1)} %convert_reduce_fusion, s32[16,8,32,1]{2,3,1,0:T(1,128)} %param.10, s32[]{:T(128)S(6)} %select_n.6, s32[]{:T(128)S(6)} %select_n.7), kind=kLoop, calls=%fused_computation.7 | loop fusion | flops 96 | bytes 392 | tf_op jit(solution)/shard_map/add | solution.py:346
  31.0 9.5 %all-to-all-done = bf16[16,512,128]{2,1,0:T(8,128)(2,1)S(1)} async-done(((bf16[16,512,128]{2,1,0:T(8,128)(2,1)}), bf16[16,512,128]{2,1,0:T(8,128)(2,1)S(1)}, u32[]{:S(2)}, u32[]{:S(2)}) %all-to-all-start) | async-done | bytes 2097184 | tf_op jit(solution)/shard_map/all_to_all | solution.py:341
  40.5 0.0 copy-start
  40.5 1.7 %phases.1 = (bf16[2,128,2048]{2,1,0:T(8,128)(2,1)S(1)}, bf16[16,4096]{1,0:T(8,128)(2,1)S(1)}, bf16[16,4096]{1,0:T(8,128)(2,1)S(1)}, bf16[64,1792]{1,0:T(8,128)(2,1)S(1)}) custom-call(s32[32]{0:T(128)S(1)} %minimum_add_fusion.slots, bf16[64,128,128]{2,1,0:T(8,128)(2,1)S(1)} %bitcast.21, bf16[64,1792]{1,0:T(8,128)(2,1)} %get-tuple-element.16.far_weights), custom_call_target="tpu_custom_call" | custom-call | tf_op jit(solution)/shard_map/phases/pallas_call | solution.py:363
  42.3 2.0 %collective-permute-start = (bf16[16,4096]{1,0:T(8,128)(2,1)S(1)}, bf16[16,4096]{1,0:T(8,128)(2,1)S(1)}, u32[]{:S(2)}, u32[]{:S(2)}) collective-permute-start(bf16[16,4096]{1,0:T(8,128)(2,1)S(1)} %get-tuple-element.17), channel_id=1, source_target_pairs={{0,1},{1,2},{2,3},{3,4},{4,5},{5,6},{6,7},{7,0},{8,9},{9,10},{10,1... | collective-permute-start | bytes 393224 | tf_op jit(solution)/shard_map/ppermute | solution.py:377
  44.2 2.8 %collective-permute-start.1 = (bf16[16,4096]{1,0:T(8,128)(2,1)S(1)}, bf16[16,4096]{1,0:T(8,128)(2,1)S(1)}, u32[]{:S(2)}, u32[]{:S(2)}) collective-permute-start(bf16[16,4096]{1,0:T(8,128)(2,1)S(1)} %get-tuple-element.18), channel_id=1, source_target_pairs={{1,0},{2,1},{3,2},{4,3},{5,4},{6,5},{7,6},{0,7},{9,8},{10,9},{11,1... | collective-permute-start | bytes 393224 | tf_op jit(solution)/shard_map/ppermute | solution.py:378
  47.0 0.0 copy-done
  47.0 8.8 %main.1.partial = f32[128,4096]{1,0:T(8,128)} custom-call(bf16[2,128,2048]{2,1,0:T(8,128)(2,1)S(1)} %get-tuple-element.20.planes, bf16[64,1792]{1,0:T(8,128)(2,1)S(1)} %get-tuple-element.21.refs_0_, bf16[64,1792]{1,0:T(8,128)(2,1)S(1)} %get-tuple-element.22.refs_1_, bf16[64,1792]{1,0:T(8,128)(2,1)S(1)} %get-tuple-element.23.refs_2_, ...), custom_call_target="tpu_custom_call" | custom-call | flops 11000000512 | bytes 8000000 | tf_op jit(solution)/shard_map/main/pallas_call | solution.py:381
  55.8 0.0 collective-permute-done.above
  55.9 0.0 collective-permute-done.1.below
  55.9 2.9 %rim.1 = f32[128,4096]{1,0:T(8,128)} custom-call(s32[2]{0:T(128)S(1)} %add_convert_fusion.inner, bf16[16,4096]{1,0:T(8,128)(2,1)S(1)} %collective-permute-done.above, bf16[16,4096]{1,0:T(8,128)(2,1)S(1)} %collective-permute-done.1.below, bf16[2,96,384]{2,1,0:T(8,128)(2,1)S(1)} %get-tuple-element.19.weights, ...), custom_call_target="tpu_custom_call", output_to_operand_aliasing={{}: (4, {})} | custom-call | tf_op jit(solution)/shard_map/rim/pallas_call | solution.py:394
Async XLA Ops:
  4.6 6.3 %copy-start.1 = (f32[40,2688]{1,0:T(8,128)S(1)}, f32[40,2688]{1,0:T(8,128)}, u32[]{:S(2)}) copy-start(f32[40,2688]{1,0:T(8,128)} %constant.23.clone) | copy-start | bytes 1290244
  4.6 6.3 %copy-start.2 = (f32[1,40,6]{1,0,2:T(1,128)S(1)}, f32[1,40,6]{1,0,2:T(1,128)}, u32[]{:S(2)}) copy-start(f32[1,40,6]{1,0,2:T(1,128)} %param.9) | copy-start | bytes 2884
  4.7 35.9 %all-to-all-start = ((bf16[16,512,128]{2,1,0:T(8,128)(2,1)}), bf16[16,512,128]{2,1,0:T(8,128)(2,1)S(1)}, u32[]{:S(2)}, u32[]{:S(2)}) async-start(bf16[16,512,128]{2,1,0:T(8,128)(2,1)} %bitcast.23), calls=%async_computation | async-start | bytes 4194304 | tf_op jit(solution)/shard_map/all_to_all | solution.py:341
  40.5 6.5 %copy-start = (f32[1,128,4096]{2,1,0:T(8,128)S(1)}, f32[1,128,4096]{2,1,0:T(8,128)}, u32[]{:S(2)}) copy-start(f32[1,128,4096]{2,1,0:T(8,128)} %param.7) | copy-start | bytes 6291460
  42.3 13.6 %collective-permute-start = (bf16[16,4096]{1,0:T(8,128)(2,1)S(1)}, bf16[16,4096]{1,0:T(8,128)(2,1)S(1)}, u32[]{:S(2)}, u32[]{:S(2)}) collective-permute-start(bf16[16,4096]{1,0:T(8,128)(2,1)S(1)} %get-tuple-element.17), channel_id=1, source_target_pairs={{0,1},{1,2},{2,3},{3,4},{4,5},{5,6},{6,7},{7,0},{8,9},{9,10},{10,1... | collective-permute-start | bytes 393224 | tf_op jit(solution)/shard_map/ppermute | solution.py:377
  44.2 11.6 %collective-permute-start.1 = (bf16[16,4096]{1,0:T(8,128)(2,1)S(1)}, bf16[16,4096]{1,0:T(8,128)(2,1)S(1)}, u32[]{:S(2)}, u32[]{:S(2)}) collective-permute-start(bf16[16,4096]{1,0:T(8,128)(2,1)S(1)} %get-tuple-element.18), channel_id=1, source_target_pairs={{1,0},{2,1},{3,2},{4,3},{5,4},{6,5},{7,6},{0,7},{9,8},{10,9},{11,1... | collective-permute-start | bytes 393224 | tf_op jit(solution)/shard_map/ppermute | solution.py:378

commit v5 on v4

--- a/solution.py
+++ b/solution.py
@@ -166,9 +166,7 @@
     return (column == home).astype(jnp.float32).astype(jnp.bfloat16)
 
 
-def phase_kernel(slots, tiles, far_weights, planes, top, bottom, near_weights, sem):
-    copy = pltpu.make_async_copy(far_weights, near_weights, sem)
-    copy.start()
+def phase_kernel(slots, tiles, planes, top, bottom):
     split = apart(False)
     for pair in range(16):
         both = jnp.concatenate([tiles[slots[2 * pair]], tiles[slots[2 * pair + 1]]], axis=1)
@@ -179,7 +177,6 @@
             at = slice(phase * 2048 + pair * TS, phase * 2048 + (pair + 1) * TS)
             top[:, at] = piece[:EDGE]
             bottom[:, at] = piece[TS - EDGE :]
-    copy.wait()
 
 
 def fold(parts, first, rows):
@@ -271,7 +268,9 @@
         out[at, columns] = science[at, columns] - model
 
 
-def rim_kernel(inner, above, below, weights, partial, out, shifted, ends, sems):
+def rim_kernel(inner, above, below, far_weights, partial, out, shifted, ends, weights, sems, weights_sem):
+    copy = pltpu.make_async_copy(far_weights, weights, weights_sem)
+    copy.start()
     zero = jnp.zeros((EDGE, TS), jnp.bfloat16)
     rows = [pl.ds(0, EDGE), pl.ds(ROWS - EDGE, EDGE)]
     for number in range(2):
@@ -287,6 +286,8 @@
             lag = index - HALF
             for i, tile in enumerate(shifted_by(near[lag % 2], lag // 2)):
                 shifted[number, index, :, i * TS : (i + 1) * TS] = tile
+    copy.wait()
+    for number in range(2):
         for first in range(0, 16, 4):
             lags = shifted[number, :, :, first * TS : (first + 4) * TS].reshape(K_EDGE, 4 * TS)
             parts = jnp.dot(weights[number, :, :K_EDGE], lags, preferred_element_type=jnp.float32)
@@ -349,9 +350,8 @@
     *main, edge = pl.pallas_call(
         weights_kernel,
         out_shape=(
-            *([jax.ShapeDtypeStruct((SIDE, K_PAD), jnp.bfloat16)] * 5),
-            pltpu.HBM((SIDE, K_PAD), jnp.bfloat16),
-            jax.ShapeDtypeStruct((2, 6 * EDGE, K_EDGE_PAD), jnp.bfloat16),
+            *([jax.ShapeDtypeStruct((SIDE, K_PAD), jnp.bfloat16)] * 6),
+            pltpu.HBM((2, 6 * EDGE, K_EDGE_PAD), jnp.bfloat16),
         ),
         in_specs=[scalars, whole],
         out_specs=(whole,) * 7,
@@ -360,19 +360,17 @@
         name="weights",
     )(amp_id.reshape(1), moments)
 
-    planes, top, bottom, main[5] = pl.pallas_call(
+    planes, top, bottom = pl.pallas_call(
         phase_kernel,
         out_shape=(
             jax.ShapeDtypeStruct((2, ROWS, 2048), jnp.bfloat16),
             *([jax.ShapeDtypeStruct((EDGE, 4096), jnp.bfloat16)] * 2),
-            jax.ShapeDtypeStruct((SIDE, K_PAD), jnp.bfloat16),
         ),
-        in_specs=[scalars, whole, pl.BlockSpec(memory_space=pl.ANY)],
-        out_specs=(whole,) * 4,
-        scratch_shapes=[pltpu.SemaphoreType.DMA],
+        in_specs=[scalars, whole],
+        out_specs=(whole,) * 3,
         compiler_params=pltpu.CompilerParams(vmem_limit_bytes=8 * MIB),
         name="phases",
-    )(slots, tiles, far(main[5]))
+    )(slots, tiles)
     down = [(i, (i + 1) % 8) for i in range(8)]
     above = lax.ppermute(bottom, "amp", down)
     below = lax.ppermute(top, "amp", [(b, a) for a, b in down])
@@ -393,18 +391,20 @@
     inner = jnp.stack([amp_id > 0, amp_id < 7]).astype(jnp.int32)
     result = pl.pallas_call(
         rim_kernel,
-        in_specs=[scalars, whole, whole, whole, pl.BlockSpec(memory_space=pl.ANY)],
+        in_specs=[scalars, whole, whole] + [pl.BlockSpec(memory_space=pl.ANY)] * 2,
         out_specs=pl.BlockSpec(memory_space=pl.ANY),
         scratch_shapes=[
             pltpu.VMEM((2, LAGS, EDGE, 2048), jnp.bfloat16),
             pltpu.VMEM((2, EDGE, 4096), jnp.float32),
+            pltpu.VMEM((2, 6 * EDGE, K_EDGE_PAD), jnp.bfloat16),
             pltpu.SemaphoreType.DMA((2, 2)),
+            pltpu.SemaphoreType.DMA,
         ],
         out_shape=jax.ShapeDtypeStruct((ROWS, 4096), jnp.float32),
         input_output_aliases={4: 0},
         compiler_params=pltpu.CompilerParams(vmem_limit_bytes=10 * MIB),
         name="rim",
-    )(inner, above, below, edge, partial)
+    )(inner, above, below, far(edge), partial)
     return result[None]
 
 

time: 59.6 us -> 59.8 us (level)
    pallas_call x1, Pallas kernels: 2.89 us -> 3.79 us  [per_device(): pl.pallas_call(rim_kernel, in_specs=[scalars, whole, whole] + [pl.BlockSp...]
    pallas_call x1, Pallas kernels: 1.72 us -> 0.99 us  [per_device(): pl.pallas_call(phase_kernel, out_shape=(jax.ShapeDtypeStruct((2, ROWS, 20...]
where the time goes in v5:
time: 59.8 us; the launch traced here: 58.9 us
  Pallas kernels  36.2 us (61%)
  starting transfers between devices  11.1 us (19%)
  waiting for transfers between devices  9.57 us (16%)
  other arithmetic  0.99 us (2%)
  local copies, waits for them, and re-layouts  0.67 us (1%)
    pallas_call x1, Pallas kernels, per_device(): pl.pallas_call(weights_kernel, out_shape=(*[jax.ShapeDtypeStruct((SIDE, K...  18.1 us
    all_to_all x1, waiting for transfers between devices, per_device(): lax.all_to_all(send.reshape(16, CAP * TS, TS), 'ccd', 0, 0, tiled=True)  9.57 us
    pallas_call x1, Pallas kernels, per_device(): pl.pallas_call(main_kernel, grid=(4096 // (2 * BLOCK),), in_specs=[whole]...  8.84 us
    all_to_all x1, starting transfers between devices, per_device(): lax.all_to_all(send.reshape(16, CAP * TS, TS), 'ccd', 0, 0, tiled=True)  6.28 us
    pallas_call x1, Pallas kernels, per_device(): pl.pallas_call(cut_kernel, grid=(16 * CAP // CUT,), out_shape=pltpu.HBM((...  4.55 us
    pallas_call x1, Pallas kernels, per_device(): pl.pallas_call(rim_kernel, in_specs=[scalars, whole, whole] + [pl.BlockSp...  3.79 us
    ppermute x1, starting transfers between devices, per_device(): below = lax.ppermute(top, 'amp', [(b, a) for a, b in down])  2.8 us
    ppermute x1, starting transfers between devices, per_device(): above = lax.ppermute(bottom, 'amp', down)  1.98 us
  transfers between devices with their start and end apart: 3, of which 1 were waited for; matrix products, arithmetic and copies ran while one was open for 3% of the time, Pallas kernels for 46%

profile of v5, /device:TPU:2, one launch (start us, length us, event | category | flops | bytes accessed | tf_op | source)
XLA Modules:
  0.0 58.9 jit_solution(5624686162273738766)
XLA Ops:
  0.0 0.1 pad_add_fusion.here
  0.1 4.6 %cut.1 = bf16[64,128,128]{2,1,0:T(8,128)(2,1)} custom-call(s32[2]{0:T(128)S(1)} %pad_add_fusion.here, s32[16,8,32]{2,1,0:T(8,128)} %bitcast.26, s32[16,8,32]{2,1,0:T(8,128)} %numbers.1, s32[16,8,2,32]{3,2,1,0:T(2,128)} %bitcast.25, f32[4,256,256]{2,1,0:T(8,128)} %bitcast.24), custom_call_target="tpu_custom_call" | custom-call | tf_op jit(solution)/shard_map/cut/pallas_call | solution.py:316
  4.6 0.0 copy-start.1
  4.7 0.0 copy-start.2
  4.7 6.3 %all-to-all-start = ((bf16[16,512,128]{2,1,0:T(8,128)(2,1)}), bf16[16,512,128]{2,1,0:T(8,128)(2,1)S(1)}, u32[]{:S(2)}, u32[]{:S(2)}) async-start(bf16[16,512,128]{2,1,0:T(8,128)(2,1)} %bitcast.23), calls=%async_computation | async-start | bytes 4194304 | tf_op jit(solution)/shard_map/all_to_all | solution.py:342
  11.0 0.0 copy-done.1
  11.0 0.0 copy-done.2
  11.0 0.3 convolution_bitcast_fusion.moments
  11.3 18.1 %weights.1 = (bf16[64,1792]{1,0:T(8,128)(2,1)S(1)}, bf16[64,1792]{1,0:T(8,128)(2,1)S(1)}, bf16[64,1792]{1,0:T(8,128)(2,1)S(1)}, bf16[64,1792]{1,0:T(8,128)(2,1)S...) custom-call(s32[1]{0:T(128)} %bitcast.3.amp, ...), custom_call_target="tpu_custom_call" | custom-call | flops 50000000 | bytes 2000000 | tf_op jit(solution)/shard_map/weights/pallas_call | solution.py:350
  29.4 0.1 add_convert_fusion.inner
  29.5 0.7 %dynamic-slice_bitcast_fusion = s32[32]{0:T(128)S(1)} fusion(s32[16,8,32,1]{2,3,1,0:T(1,128)} %param.10, s32[]{:T(128)S(6)} %select_n.6, s32[]{:T(128)S(6)} %select_n.7), kind=kLoop, calls=%fused_computation.8 | loop fusion | bytes 264 | tf_op jit(solution)/shard_map/squeeze | solution.py:345
  30.1 0.2 convert_reduce_fusion
  30.3 0.7 %minimum_add_fusion.slots = s32[32]{0:T(128)S(1)} fusion(s32[32]{0:T(128)S(1)} %convert_reduce_fusion, s32[16,8,32,1]{2,3,1,0:T(1,128)} %param.10, s32[]{:T(128)S(6)} %select_n.6, s32[]{:T(128)S(6)} %select_n.7), kind=kLoop, calls=%fused_computation.7 | loop fusion | flops 96 | bytes 392 | tf_op jit(solution)/shard_map/add | solution.py:347
  31.0 9.6 %all-to-all-done = bf16[16,512,128]{2,1,0:T(8,128)(2,1)S(1)} async-done(((bf16[16,512,128]{2,1,0:T(8,128)(2,1)}), bf16[16,512,128]{2,1,0:T(8,128)(2,1)S(1)}, u32[]{:S(2)}, u32[]{:S(2)}) %all-to-all-start) | async-done | bytes 2097184 | tf_op jit(solution)/shard_map/all_to_all | solution.py:342
  40.5 0.0 copy-start
  40.5 1.0 %phases.1 = (bf16[2,128,2048]{2,1,0:T(8,128)(2,1)S(1)}, bf16[16,4096]{1,0:T(8,128)(2,1)S(1)}, bf16[16,4096]{1,0:T(8,128)(2,1)S(1)}) custom-call(s32[32]{0:T(128)S(1)} %minimum_add_fusion.slots, bf16[64,128,128]{2,1,0:T(8,128)(2,1)S(1)} %bitcast.21), custom_call_target="tpu_custom_call" | custom-call | tf_op jit(solution)/shard_map/phases/pallas_call | solution.py:363
  41.5 2.0 %collective-permute-start = (bf16[16,4096]{1,0:T(8,128)(2,1)S(1)}, bf16[16,4096]{1,0:T(8,128)(2,1)S(1)}, u32[]{:S(2)}, u32[]{:S(2)}) collective-permute-start(bf16[16,4096]{1,0:T(8,128)(2,1)S(1)} %get-tuple-element.15), channel_id=1, source_target_pairs={{0,1},{1,2},{2,3},{3,4},{4,5},{5,6},{6,7},{7,0},{8,9},{9,10},{10,1... | collective-permute-start | bytes 393224 | tf_op jit(solution)/shard_map/ppermute | solution.py:375
  43.5 2.8 %collective-permute-start.1 = (bf16[16,4096]{1,0:T(8,128)(2,1)S(1)}, bf16[16,4096]{1,0:T(8,128)(2,1)S(1)}, u32[]{:S(2)}, u32[]{:S(2)}) collective-permute-start(bf16[16,4096]{1,0:T(8,128)(2,1)S(1)} %get-tuple-element.16), channel_id=1, source_target_pairs={{1,0},{2,1},{3,2},{4,3},{5,4},{6,5},{7,6},{0,7},{9,8},{10,9},{11,1... | collective-permute-start | bytes 393224 | tf_op jit(solution)/shard_map/ppermute | solution.py:376
  46.3 0.0 copy-done
  46.3 8.8 %main.1.partial = f32[128,4096]{1,0:T(8,128)} custom-call(bf16[2,128,2048]{2,1,0:T(8,128)(2,1)S(1)} %get-tuple-element.18.planes, bf16[64,1792]{1,0:T(8,128)(2,1)S(1)} %get-tuple-element.19.refs_0_, bf16[64,1792]{1,0:T(8,128)(2,1)S(1)} %get-tuple-element.20.refs_1_, bf16[64,1792]{1,0:T(8,128)(2,1)S(1)} %get-tuple-element.21.refs_2_, ...), custom_call_target="tpu_custom_call" | custom-call | flops 11000000512 | bytes 8000000 | tf_op jit(solution)/shard_map/main/pallas_call | solution.py:379
  55.2 0.0 collective-permute-done.above
  55.2 0.0 collective-permute-done.1.below
  55.2 3.8 %rim.1 = f32[128,4096]{1,0:T(8,128)} custom-call(s32[2]{0:T(128)S(1)} %add_convert_fusion.inner, bf16[16,4096]{1,0:T(8,128)(2,1)S(1)} %collective-permute-done.above, bf16[16,4096]{1,0:T(8,128)(2,1)S(1)} %collective-permute-done.1.below, bf16[2,96,384]{2,1,0:T(8,128)(2,1)} %get-tuple-element.17.far_weights, ...), custom_call_target="tpu_custom_call", output_to_operand_aliasing={{}: (4, {})} | custom-call | tf_op jit(solution)/shard_map/rim/pallas_call | solution.py:392
Async XLA Ops:
  4.6 6.3 %copy-start.1 = (f32[40,2688]{1,0:T(8,128)S(1)}, f32[40,2688]{1,0:T(8,128)}, u32[]{:S(2)}) copy-start(f32[40,2688]{1,0:T(8,128)} %constant.23.clone) | copy-start | bytes 1290244
  4.7 6.3 %copy-start.2 = (f32[1,40,6]{1,0,2:T(1,128)S(1)}, f32[1,40,6]{1,0,2:T(1,128)}, u32[]{:S(2)}) copy-start(f32[1,40,6]{1,0,2:T(1,128)} %param.9) | copy-start | bytes 2884
  4.7 35.9 %all-to-all-start = ((bf16[16,512,128]{2,1,0:T(8,128)(2,1)}), bf16[16,512,128]{2,1,0:T(8,128)(2,1)S(1)}, u32[]{:S(2)}, u32[]{:S(2)}) async-start(bf16[16,512,128]{2,1,0:T(8,128)(2,1)} %bitcast.23), calls=%async_computation | async-start | bytes 4194304 | tf_op jit(solution)/shard_map/all_to_all | solution.py:342
  40.5 5.8 %copy-start = (f32[1,128,4096]{2,1,0:T(8,128)S(1)}, f32[1,128,4096]{2,1,0:T(8,128)}, u32[]{:S(2)}) copy-start(f32[1,128,4096]{2,1,0:T(8,128)} %param.7) | copy-start | bytes 6291460
  41.5 13.6 %collective-permute-start = (bf16[16,4096]{1,0:T(8,128)(2,1)S(1)}, bf16[16,4096]{1,0:T(8,128)(2,1)S(1)}, u32[]{:S(2)}, u32[]{:S(2)}) collective-permute-start(bf16[16,4096]{1,0:T(8,128)(2,1)S(1)} %get-tuple-element.15), channel_id=1, source_target_pairs={{0,1},{1,2},{2,3},{3,4},{4,5},{5,6},{6,7},{7,0},{8,9},{9,10},{10,1... | collective-permute-start | bytes 393224 | tf_op jit(solution)/shard_map/ppermute | solution.py:375
  43.5 11.6 %collective-permute-start.1 = (bf16[16,4096]{1,0:T(8,128)(2,1)S(1)}, bf16[16,4096]{1,0:T(8,128)(2,1)S(1)}, u32[]{:S(2)}, u32[]{:S(2)}) collective-permute-start(bf16[16,4096]{1,0:T(8,128)(2,1)S(1)} %get-tuple-element.16), channel_id=1, source_target_pairs={{1,0},{2,1},{3,2},{4,3},{5,4},{6,5},{7,6},{0,7},{9,8},{10,9},{11,1... | collective-permute-start | bytes 393224 | tf_op jit(solution)/shard_map/ppermute | solution.py:376

commit v6 on v4

--- a/solution.py
+++ b/solution.py
@@ -166,9 +166,7 @@
     return (column == home).astype(jnp.float32).astype(jnp.bfloat16)
 
 
-def phase_kernel(slots, tiles, far_weights, planes, top, bottom, near_weights, sem):
-    copy = pltpu.make_async_copy(far_weights, near_weights, sem)
-    copy.start()
+def phase_kernel(slots, tiles, planes, top, bottom):
     split = apart(False)
     for pair in range(16):
         both = jnp.concatenate([tiles[slots[2 * pair]], tiles[slots[2 * pair + 1]]], axis=1)
@@ -179,7 +177,6 @@
             at = slice(phase * 2048 + pair * TS, phase * 2048 + (pair + 1) * TS)
             top[:, at] = piece[:EDGE]
             bottom[:, at] = piece[TS - EDGE :]
-    copy.wait()
 
 
 def fold(parts, first, rows):
@@ -229,7 +226,8 @@
 
 
 def main_kernel(planes, *refs):
-    weights, (science, out, even, odd) = refs[:6], refs[6:]
+    far_weights, (science, out, even, odd, held, sem) = refs[5], refs[6:]
+    weights = (*refs[:5], held)
     step = pl.program_id(0)
 
     def shift(first, buffer):
@@ -257,7 +255,10 @@
 
     @pl.when(step == 0)
     def _():
+        copy = pltpu.make_async_copy(far_weights, held, sem)
+        copy.start()
         shift(0, even)
+        copy.wait()
 
     first = step * 2 * TILES
     shift(first + TILES, odd)
@@ -360,19 +361,17 @@
         name="weights",
     )(amp_id.reshape(1), moments)
 
-    planes, top, bottom, main[5] = pl.pallas_call(
+    planes, top, bottom = pl.pallas_call(
         phase_kernel,
         out_shape=(
             jax.ShapeDtypeStruct((2, ROWS, 2048), jnp.bfloat16),
             *([jax.ShapeDtypeStruct((EDGE, 4096), jnp.bfloat16)] * 2),
-            jax.ShapeDtypeStruct((SIDE, K_PAD), jnp.bfloat16),
         ),
-        in_specs=[scalars, whole, pl.BlockSpec(memory_space=pl.ANY)],
-        out_specs=(whole,) * 4,
-        scratch_shapes=[pltpu.SemaphoreType.DMA],
+        in_specs=[scalars, whole],
+        out_specs=(whole,) * 3,
         compiler_params=pltpu.CompilerParams(vmem_limit_bytes=8 * MIB),
         name="phases",
-    )(slots, tiles, far(main[5]))
+    )(slots, tiles)
     down = [(i, (i + 1) % 8) for i in range(8)]
     above = lax.ppermute(bottom, "amp", down)
     below = lax.ppermute(top, "amp", [(b, a) for a, b in down])
@@ -381,14 +380,15 @@
     partial = pl.pallas_call(
         main_kernel,
         grid=(4096 // (2 * BLOCK),),
-        in_specs=[whole] * 7 + [columns],
+        in_specs=[whole] * 6 + [pl.BlockSpec(memory_space=pl.ANY), columns],
         out_specs=columns,
-        scratch_shapes=[pltpu.VMEM((LAGS, ROWS, WIDE), jnp.bfloat16)] * 2,
+        scratch_shapes=[pltpu.VMEM((LAGS, ROWS, WIDE), jnp.bfloat16)] * 2
+        + [pltpu.VMEM((SIDE, K_PAD), jnp.bfloat16), pltpu.SemaphoreType.DMA],
         out_shape=jax.ShapeDtypeStruct((ROWS, 4096), jnp.float32),
         compiler_params=pltpu.CompilerParams(vmem_limit_bytes=12 * MIB),
         cost_estimate=pl.CostEstimate(flops=11_000_000_000, bytes_accessed=8_000_000, transcendentals=0),
         name="main",
-    )(planes, *main, science[0])
+    )(planes, *main[:5], far(main[5]), science[0])
 
     inner = jnp.stack([amp_id > 0, amp_id < 7]).astype(jnp.int32)
     result = pl.pallas_call(

time: 59.6 us -> 59.6 us (level)
    pallas_call x1, Pallas kernels: 1.72 us -> 0.99 us  [per_device(): pl.pallas_call(phase_kernel, out_shape=(jax.ShapeDtypeStruct((2, ROWS, 20...]
    pallas_call x1, Pallas kernels: 8.81 us -> 9.46 us  [per_device(): pl.pallas_call(main_kernel, grid=(4096 // (2 * BLOCK),), in_specs=[whole]...]
  transfers between devices with their start and end apart: 3 -> 3, of which waited for: 1 -> 1; matrix products, arithmetic and copies ran while one was open for 3% -> 3% of each run, Pallas kernels for 46% -> 47%
where the time goes in v6:
time: 59.6 us; the launch traced here: 58.7 us
  Pallas kernels  36 us (60%)
  starting transfers between devices  11.1 us (19%)
  waiting for transfers between devices  9.55 us (16%)
  other arithmetic  0.99 us (2%)
  local copies, waits for them, and re-layouts  0.67 us (1%)
    pallas_call x1, Pallas kernels, per_device(): pl.pallas_call(weights_kernel, out_shape=(*[jax.ShapeDtypeStruct((SIDE, K...  18.1 us
    all_to_all x1, waiting for transfers between devices, per_device(): lax.all_to_all(send.reshape(16, CAP * TS, TS), 'ccd', 0, 0, tiled=True)  9.55 us
    pallas_call x1, Pallas kernels, per_device(): pl.pallas_call(main_kernel, grid=(4096 // (2 * BLOCK),), in_specs=[whole]...  9.46 us
    all_to_all x1, starting transfers between devices, per_device(): lax.all_to_all(send.reshape(16, CAP * TS, TS), 'ccd', 0, 0, tiled=True)  6.28 us
    pallas_call x1, Pallas kernels, per_device(): pl.pallas_call(cut_kernel, grid=(16 * CAP // CUT,), out_shape=pltpu.HBM((...  4.55 us
    pallas_call x1, Pallas kernels, per_device(): pl.pallas_call(rim_kernel, in_specs=[scalars, whole, whole, whole, pl.Blo...  2.89 us
    ppermute x1, starting transfers between devices, per_device(): below = lax.ppermute(top, 'amp', [(b, a) for a, b in down])  2.8 us
    ppermute x1, starting transfers between devices, per_device(): above = lax.ppermute(bottom, 'amp', down)  1.99 us
  transfers between devices with their start and end apart: 3, of which 1 were waited for; matrix products, arithmetic and copies ran while one was open for 3% of the time, Pallas kernels for 47%

profile of v6, /device:TPU:2, one launch (start us, length us, event | category | flops | bytes accessed | tf_op | source)
XLA Modules:
  0.0 58.7 jit_solution(13295926821377954834)
XLA Ops:
  0.0 0.1 pad_add_fusion.here
  0.1 4.6 %cut.1 = bf16[64,128,128]{2,1,0:T(8,128)(2,1)} custom-call(s32[2]{0:T(128)S(1)} %pad_add_fusion.here, s32[16,8,32]{2,1,0:T(8,128)} %bitcast.26, s32[16,8,32]{2,1,0:T(8,128)} %numbers.1, s32[16,8,2,32]{3,2,1,0:T(2,128)} %bitcast.25, f32[4,256,256]{2,1,0:T(8,128)} %bitcast.24), custom_call_target="tpu_custom_call" | custom-call | tf_op jit(solution)/shard_map/cut/pallas_call | solution.py:316
  4.6 0.0 copy-start.1
  4.6 0.0 copy-start.2
  4.7 6.3 %all-to-all-start = ((bf16[16,512,128]{2,1,0:T(8,128)(2,1)}), bf16[16,512,128]{2,1,0:T(8,128)(2,1)S(1)}, u32[]{:S(2)}, u32[]{:S(2)}) async-start(bf16[16,512,128]{2,1,0:T(8,128)(2,1)} %bitcast.23), calls=%async_computation | async-start | bytes 4194304 | tf_op jit(solution)/shard_map/all_to_all | solution.py:342
  11.0 0.0 copy-done.1
  11.0 0.0 copy-done.2
  11.0 0.3 convolution_bitcast_fusion.moments
  11.3 18.1 %weights.1 = (bf16[64,1792]{1,0:T(8,128)(2,1)S(1)}, bf16[64,1792]{1,0:T(8,128)(2,1)S(1)}, bf16[64,1792]{1,0:T(8,128)(2,1)S(1)}, bf16[64,1792]{1,0:T(8,128)(2,1)S...) custom-call(s32[1]{0:T(128)} %bitcast.3.amp, ...), custom_call_target="tpu_custom_call" | custom-call | flops 50000000 | bytes 2000000 | tf_op jit(solution)/shard_map/weights/pallas_call | solution.py:350
  29.4 0.1 add_convert_fusion.inner
  29.5 0.7 %dynamic-slice_bitcast_fusion = s32[32]{0:T(128)S(1)} fusion(s32[16,8,32,1]{2,3,1,0:T(1,128)} %param.10, s32[]{:T(128)S(6)} %select_n.6, s32[]{:T(128)S(6)} %select_n.7), kind=kLoop, calls=%fused_computation.8 | loop fusion | bytes 264 | tf_op jit(solution)/shard_map/squeeze | solution.py:345
  30.1 0.2 convert_reduce_fusion
  30.3 0.7 %minimum_add_fusion.slots = s32[32]{0:T(128)S(1)} fusion(s32[32]{0:T(128)S(1)} %convert_reduce_fusion, s32[16,8,32,1]{2,3,1,0:T(1,128)} %param.10, s32[]{:T(128)S(6)} %select_n.6, s32[]{:T(128)S(6)} %select_n.7), kind=kLoop, calls=%fused_computation.7 | loop fusion | flops 96 | bytes 392 | tf_op jit(solution)/shard_map/add | solution.py:347
  31.0 9.5 %all-to-all-done = bf16[16,512,128]{2,1,0:T(8,128)(2,1)S(1)} async-done(((bf16[16,512,128]{2,1,0:T(8,128)(2,1)}), bf16[16,512,128]{2,1,0:T(8,128)(2,1)S(1)}, u32[]{:S(2)}, u32[]{:S(2)}) %all-to-all-start) | async-done | bytes 2097184 | tf_op jit(solution)/shard_map/all_to_all | solution.py:342
  40.5 0.0 copy-start
  40.5 1.0 %phases.1 = (bf16[2,128,2048]{2,1,0:T(8,128)(2,1)S(1)}, bf16[16,4096]{1,0:T(8,128)(2,1)S(1)}, bf16[16,4096]{1,0:T(8,128)(2,1)S(1)}) custom-call(s32[32]{0:T(128)S(1)} %minimum_add_fusion.slots, bf16[64,128,128]{2,1,0:T(8,128)(2,1)S(1)} %bitcast.21), custom_call_target="tpu_custom_call" | custom-call | tf_op jit(solution)/shard_map/phases/pallas_call | solution.py:364
  41.5 2.0 %collective-permute-start = (bf16[16,4096]{1,0:T(8,128)(2,1)S(1)}, bf16[16,4096]{1,0:T(8,128)(2,1)S(1)}, u32[]{:S(2)}, u32[]{:S(2)}) collective-permute-start(bf16[16,4096]{1,0:T(8,128)(2,1)S(1)} %get-tuple-element.15), channel_id=1, source_target_pairs={{0,1},{1,2},{2,3},{3,4},{4,5},{5,6},{6,7},{7,0},{8,9},{9,10},{10,1... | collective-permute-start | bytes 393224 | tf_op jit(solution)/shard_map/ppermute | solution.py:376
  43.5 2.8 %collective-permute-start.1 = (bf16[16,4096]{1,0:T(8,128)(2,1)S(1)}, bf16[16,4096]{1,0:T(8,128)(2,1)S(1)}, u32[]{:S(2)}, u32[]{:S(2)}) collective-permute-start(bf16[16,4096]{1,0:T(8,128)(2,1)S(1)} %get-tuple-element.16), channel_id=1, source_target_pairs={{1,0},{2,1},{3,2},{4,3},{5,4},{6,5},{7,6},{0,7},{9,8},{10,9},{11,1... | collective-permute-start | bytes 393224 | tf_op jit(solution)/shard_map/ppermute | solution.py:377
  46.3 0.0 copy-done
  46.3 9.5 %main.1.partial = f32[128,4096]{1,0:T(8,128)} custom-call(bf16[2,128,2048]{2,1,0:T(8,128)(2,1)S(1)} %get-tuple-element.18.planes, bf16[64,1792]{1,0:T(8,128)(2,1)S(1)} %get-tuple-element.19.refs_0_, bf16[64,1792]{1,0:T(8,128)(2,1)S(1)} %get-tuple-element.20.refs_1_, bf16[64,1792]{1,0:T(8,128)(2,1)S(1)} %get-tuple-element.21.refs_2_, ...), custom_call_target="tpu_custom_call" | custom-call | flops 11000000512 | bytes 8000000 | tf_op jit(solution)/shard_map/main/pallas_call | solution.py:380
  55.8 0.0 collective-permute-done.above
  55.8 0.0 collective-permute-done.1.below
  55.8 2.9 %rim.1 = f32[128,4096]{1,0:T(8,128)} custom-call(s32[2]{0:T(128)S(1)} %add_convert_fusion.inner, bf16[16,4096]{1,0:T(8,128)(2,1)S(1)} %collective-permute-done.above, bf16[16,4096]{1,0:T(8,128)(2,1)S(1)} %collective-permute-done.1.below, bf16[2,96,384]{2,1,0:T(8,128)(2,1)S(1)} %get-tuple-element.17.weights, ...), custom_call_target="tpu_custom_call", output_to_operand_aliasing={{}: (4, {})} | custom-call | tf_op jit(solution)/shard_map/rim/pallas_call | solution.py:394
Async XLA Ops:
  4.6 6.3 %copy-start.1 = (f32[40,2688]{1,0:T(8,128)S(1)}, f32[40,2688]{1,0:T(8,128)}, u32[]{:S(2)}) copy-start(f32[40,2688]{1,0:T(8,128)} %constant.23.clone) | copy-start | bytes 1290244
  4.6 6.3 %copy-start.2 = (f32[1,40,6]{1,0,2:T(1,128)S(1)}, f32[1,40,6]{1,0,2:T(1,128)}, u32[]{:S(2)}) copy-start(f32[1,40,6]{1,0,2:T(1,128)} %param.9) | copy-start | bytes 2884
  4.7 35.9 %all-to-all-start = ((bf16[16,512,128]{2,1,0:T(8,128)(2,1)}), bf16[16,512,128]{2,1,0:T(8,128)(2,1)S(1)}, u32[]{:S(2)}, u32[]{:S(2)}) async-start(bf16[16,512,128]{2,1,0:T(8,128)(2,1)} %bitcast.23), calls=%async_computation | async-start | bytes 4194304 | tf_op jit(solution)/shard_map/all_to_all | solution.py:342
  40.5 5.8 %copy-start = (f32[1,128,4096]{2,1,0:T(8,128)S(1)}, f32[1,128,4096]{2,1,0:T(8,128)}, u32[]{:S(2)}) copy-start(f32[1,128,4096]{2,1,0:T(8,128)} %param.7) | copy-start | bytes 6291460
  41.5 14.3 %collective-permute-start = (bf16[16,4096]{1,0:T(8,128)(2,1)S(1)}, bf16[16,4096]{1,0:T(8,128)(2,1)S(1)}, u32[]{:S(2)}, u32[]{:S(2)}) collective-permute-start(bf16[16,4096]{1,0:T(8,128)(2,1)S(1)} %get-tuple-element.15), channel_id=1, source_target_pairs={{0,1},{1,2},{2,3},{3,4},{4,5},{5,6},{6,7},{7,0},{8,9},{9,10},{10,1... | collective-permute-start | bytes 393224 | tf_op jit(solution)/shard_map/ppermute | solution.py:376
  43.5 12.3 %collective-permute-start.1 = (bf16[16,4096]{1,0:T(8,128)(2,1)S(1)}, bf16[16,4096]{1,0:T(8,128)(2,1)S(1)}, u32[]{:S(2)}, u32[]{:S(2)}) collective-permute-start(bf16[16,4096]{1,0:T(8,128)(2,1)S(1)} %get-tuple-element.16), channel_id=1, source_target_pairs={{1,0},{2,1},{3,2},{4,3},{5,4},{6,5},{7,6},{0,7},{9,8},{10,9},{11,1... | collective-permute-start | bytes 393224 | tf_op jit(solution)/shard_map/ppermute | solution.py:377
